TPU v7x, 256 devices: a whole 4x4x8 slice. The times are simulated.
256 devices in a mesh: clus: 32 (over x, y, core), probe: 8 (over z).
Axes of the slice: x: 4, y: 4, z: 8, core: 2. Of those that a mesh axis runs over, the one named last changes fastest.
Arguments:
- probes: bfloat16 [384, 128, 128], P('clus', 'probe'), may hold values from -6 to 6
- onsite: float32 [384, 128], P('clus'), may hold values from -1.1 to 1.1
- hopping: bfloat16 [20, 384, 128, 128], P(None, 'clus'), may hold values from -0.0390625 to 0.0390625
- block_col: int32 [20, 384], P(None, 'clus'), may hold values from -1 to 383, as said below
- atom_of: int32 [384, 128], P('clus'), may hold values from 0 to 31, as said below
- bond_dir: bfloat16 [3, 20, 384], P(None, None, 'clus'), may hold values from -1 to 1, as said below
- chemical_potential: float32 [1], replicated, may hold values from -0.3 to 0.3
Outputs:
- density: float32 [384, 128], P('clus')
- filling: float32 [1], replicated
- forces: float32 [3, 12288], P(None, 'clus')
Inputs may be any that keep to these rules, and one draw needn't show every extreme that they name: `block_col`: -1 marks an empty slot. Slot (m, c) belongs to row cluster c; a live slot's column cluster lies within 12 clusters of c, and the live columns of one row cluster are distinct. In each aligned group of 12 row clusters the live slots are those with m under a count common to the group, either 20 or from 5 to 10, except columns that would fall outside the grid, which are empty. In some group, never the first or the last, every slot is live. `atom_of`: in each cluster every atom number appears for exactly four orbitals. `bond_dir`: the three components of each slot form a unit vector.
All inputs are finite; a program needn't handle non-finite values.
Results may differ from a plain program's by a relative error of at most 0.0011.
Values may be sent and summed in bfloat16 or wider, within the bound.
A program may use at most 128 MiB of HBM per device.

v0:
```python
import jax
import jax.numpy as jnp
from jax import lax
from jax.sharding import PartitionSpec as P

ATOMS = 32
REACH = 12
PROBE_VECTORS = 128
ORDER = 4


DECAY = 50.0
SMEARING_TEMP = 0.1
quad_nodes = 64


def extended(block, sides, width):
    for axis, dim in sides:
        count = lax.axis_size(axis)
        forward = [(i, i + 1) for i in range(count - 1)]
        backward = [(target, source) for source, target in forward]
        low = lax.ppermute(
            lax.slice_in_dim(block, block.shape[dim] - width, None, axis=dim), axis, forward
        )
        high = lax.ppermute(lax.slice_in_dim(block, 0, width, axis=dim), axis, backward)
        block = jnp.concatenate([low, block, high], axis=dim)
    return block


def passed_along(array, axis, by):
    devices = lax.axis_size(axis)
    pairs = [(i, i + by) for i in range(devices) if 0 <= i + by < devices]
    return lax.ppermute(array, axis, pairs)


def expansion(chemical_potential, degree):
    node_index = jnp.arange(quad_nodes, dtype=jnp.float32)
    bond_angles = jnp.pi * (node_index + 0.5) / quad_nodes
    fermi_occupation = 1.0 / (
        1.0 + jnp.exp((jnp.cos(bond_angles) - chemical_potential) / SMEARING_TEMP)
    )
    orders = jnp.arange(degree + 1, dtype=jnp.float32)
    cosines = jnp.cos(orders[:, None] * bond_angles[None, :])
    coeffs = 2.0 / quad_nodes * jnp.sum(cosines * fermi_occupation[None, :], axis=1)
    return coeffs * jnp.where(orders == 0.0, 0.5, 1.0)


def gather_columns(source, gather_ids):
    safe_ids = jnp.minimum(gather_ids, source.shape[0] - 1)
    picked = jnp.take(source, safe_ids.reshape(-1), axis=0)
    return picked.reshape(gather_ids.shape + source.shape[1:])


def direct_terms(padded, blocks, gather_ids):
    picked = gather_columns(padded, gather_ids)
    return jnp.einsum("mrpj,mrij->rpi", picked, blocks, preferred_element_type=jnp.float32)


def spread_terms(vector_rows, blocks, target_ids, segments):
    spread = jnp.einsum("rpi,mrij->mrpj", vector_rows, blocks, preferred_element_type=jnp.float32)
    flat = spread.reshape((-1,) + spread.shape[2:])
    return jax.ops.segment_sum(flat, target_ids.reshape(-1), num_segments=segments)


def bond_sums(u_rows, v_rows, u_cols, v_cols, blocks):
    density_blocks = jnp.einsum(
        "rpi,mrpj->mrij", u_rows, v_cols, preferred_element_type=jnp.float32
    )
    density_blocks = density_blocks + jnp.einsum(
        "rpi,mrpj->mrij", v_rows, u_cols, preferred_element_type=jnp.float32
    )
    product = density_blocks * blocks.astype(jnp.float32)
    return (jnp.sum(product, axis=3), jnp.sum(product, axis=2))


def column_force(directions, col_sums, target_ids, segments):
    facing = jnp.transpose(directions.astype(jnp.float32), (1, 2, 0))
    terms = DECAY * facing[:, :, :, None] * col_sums[:, :, None, :]
    flat = terms.reshape((-1,) + terms.shape[2:])
    return jax.ops.segment_sum(flat, target_ids.reshape(-1), num_segments=segments)


def local(probes, onsite, hopping, block_col, atom_of, bond_dir, chemical_potential):
    clusters = probes.shape[0]
    offset = lax.axis_index("clus") * clusters
    orbitals = clusters * lax.axis_size("clus") * probes.shape[2]
    live_mask = block_col >= 0
    masked_hop = jnp.where(live_mask[:, :, None, None], hopping, jnp.zeros((), hopping.dtype))
    frame_ids = jnp.where(live_mask, block_col - offset + REACH, clusters + 2 * REACH)
    coeffs = expansion(chemical_potential[0], ORDER)
    probe_wide = probes.astype(jnp.float32)
    partial_sq = jnp.sum(probe_wide * probe_wide, axis=(0, 2))
    norm_sq = lax.psum(partial_sq, "clus")

    def operate(vector_b):
        padded = extended(vector_b, (("clus", 0),), REACH)
        direct = direct_terms(padded, masked_hop, frame_ids)
        carried = spread_terms(vector_b, masked_hop, frame_ids, clusters + 2 * REACH + 1)
        from_right = passed_along(carried[:REACH], "clus", -1)
        from_left = passed_along(carried[clusters + REACH : clusters + 2 * REACH], "clus", 1)
        back = carried[REACH : REACH + clusters]
        back = back + from_right
        back = back + from_left
        result = onsite[:, None, :] * vector_b.astype(jnp.float32) + direct + back
        return (result, padded)

    previous = probe_wide
    current, probe_pad = operate(probes)
    fermi_vec = coeffs[0] * previous + coeffs[1] * current
    for term_index in range(2, ORDER + 1):
        image, unused = operate(current.astype(jnp.bfloat16))
        following = 2.0 * image - previous
        fermi_vec = fermi_vec + coeffs[term_index] * following
        previous, current = (current, following)
    scale = orbitals / (norm_sq * PROBE_VECTORS)
    density_part = jnp.sum(probe_wide * fermi_vec * scale[None, :, None], axis=1)
    weighted = (fermi_vec * scale[None, :, None]).astype(jnp.bfloat16)
    weighted_pad = extended(weighted, (("clus", 0),), REACH)
    u_cols = gather_columns(weighted_pad, frame_ids)
    v_cols = gather_columns(probe_pad, frame_ids)
    row_sums, col_sums = bond_sums(weighted, probes, u_cols, v_cols, masked_hop)
    facing = jnp.transpose(bond_dir.astype(jnp.float32), (1, 2, 0))
    orbital_gradient = jnp.sum(-DECAY * facing[:, :, :, None] * row_sums[:, :, None, :], axis=0)
    col_force = column_force(bond_dir, col_sums, frame_ids, clusters + 2 * REACH + 1)
    from_right = passed_along(col_force[:REACH], "clus", -1)
    from_left = passed_along(col_force[clusters + REACH : clusters + 2 * REACH], "clus", 1)
    orbital_gradient = orbital_gradient + col_force[REACH : REACH + clusters]
    orbital_gradient = orbital_gradient + from_right
    orbital_gradient = orbital_gradient + from_left
    atom_table = (atom_of[:, :, None] == jnp.arange(ATOMS, dtype=jnp.int32)[None, None, :]).astype(
        jnp.float32
    )
    atom_part = jnp.einsum(
        "rxb,rba->xra", orbital_gradient, atom_table, precision=lax.Precision.HIGHEST
    ).reshape(3, -1)
    density, atom_force = lax.psum((density_part, atom_part), "probe")
    filling = lax.psum(jnp.sum(density), "clus") / orbitals
    return (density, filling.reshape(1), atom_force)


def solution(mesh):
    placed = (
        P("clus", "probe", None),
        P("clus", None),
        P(None, "clus", None, None),
        P(None, "clus"),
        P("clus", None),
        P(None, None, "clus"),
        P(),
    )
    return jax.shard_map(
        local,
        mesh=mesh,
        in_specs=placed,
        out_specs=(P("clus", None), P(), P(None, "clus")),
        check_vma=False,
    )
```

profile of v0, /device:TPU:6, one launch (start us, length us, event | category | flops | bytes accessed | tf_op | source)
XLA Modules:
  0.0 356.0 jit_solution(17833078247190660412)
XLA Ops:
  0.6 4.6 %collective-permute-start.1 = (bf16[12,16,128]{2,1,0:T(8,128)(2,1)}, bf16[12,16,128]{2,1,0:T(8,128)(2,1)S(1)}, u32[]{:S(2)}, u32[]{:S(2)}) collective-permute-start(bf16[12,16,128]{2,1,0:T(8,128)(2,1)} %param.9), channel_id=1, source_target_pairs={{8,0},{16,8},{24,16},{32,24},{40,32},{48,40},{56,48},{64,56},{72,6... | collective-permute-start | bytes 147464 | tf_op jit(solution)/shard_map/ppermute | solution.py:25
  5.3 1.9 collective-permute-start
  8.8 10.7 %copy.79 = bf16[20,12,128,128]{2,3,0,1:T(8,128)(2,1)} copy(bf16[20,12,128,128]{3,2,1,0:T(8,128)(2,1)} %param.11) | data formatting | bytes 15728640 | tf_op args[2]
  19.5 4.5 %convolution_bitcast_fusion.3 = f32[20,12,16,128]{3,2,0,1:T(8,128)S(1)} fusion(bf16[12,16,128]{2,1,0:T(8,128)(2,1)S(1)} %copy-done.2, bf16[20,12,128,128]{2,3,0,1:T(8,128)(2,1)} %copy.79, pred[20,12]{0,1:T(8,128)(4,1)S(1)} %broadcast_compare_fusion), kind=kOutput, calls=%fused_computation.23 | convolution fusion | flops 129761280 | bytes 9879792 | tf_op jit(solution)/shard_map/rpi,mrij->mrpj/dot_general | solution.py:60
  24.3 9.7 %scatter_fusion = f32[37,16,128]{2,1,0:T(8,128)S(1)} fusion(f32[37,16,128]{2,1,0:T(8,128)S(1)} %broadcast.78.clone.1, s32[240]{0:T(256)S(1)} %reshape.135, f32[240,16,128]{2,1,0:T(8,128)S(1)} %bitcast.98), kind=kCustom, calls=%fused_computation.5 | custom fusion | flops 491520 | bytes 5899200 | tf_op jit(solution)/shard_map/scatter-add | solution.py:62
  34.1 1.9 collective-permute-start.3
  36.0 5.8 %collective-permute-start.2 = (f32[12,16,128]{2,1,0:T(8,128)S(1)}, f32[12,16,128]{2,1,0:T(8,128)S(1)}, u32[]{:S(2)}, u32[]{:S(2)}) collective-permute-start(f32[12,16,128]{2,1,0:T(8,128)S(1)} %get-tuple-element.16), channel_id=1, source_target_pairs={{8,0},{16,8},{24,16},{32,24},{40,32},{48,40},{56,48},{64,56},{72,6... | collective-permute-start | bytes 294920 | tf_op jit(solution)/shard_map/ppermute | solution.py:33
  46.4 4.9 %fusion.80 = (bf16[12,16,128]{2,1,0:T(8,128)(2,1)S(1)}, f32[12,16,128]{2,1,0:T(8,128)}) fusion(f32[12,16,128]{2,1,0:T(8,128)S(1)} %collective-permute-done.3, f32[12,16,128]{2,1,0:T(8,128)S(1)} %collective-permute-done.2, f32[37,16,128]{2,1,0:T(8,128)S(1)} %scatter_fusion, bf16[20,12,16,128]{3,2,1,0:T(8,128)(2,1)S(1)} %bitcast.102, ...), kind=kOutput, calls=%fused_computation.113 | convolution fusion | flops 129933312 | bytes 9345264 | tf_op jit(solution)/shard_map/mrpj,mrij->rpi/dot_general | solution.py:56
  51.8 2.4 convolution_bitcast_fusion.2
  54.2 2.9 collective-permute-start.5
  57.1 1.9 collective-permute-start.4
  59.3 9.7 %scatter_fusion.1 = f32[37,16,128]{2,1,0:T(8,128)S(1)} fusion(f32[37,16,128]{2,1,0:T(8,128)S(1)} %broadcast.78.clone, s32[240]{0:T(256)S(1)} %reshape.135, f32[240,16,128]{2,1,0:T(8,128)S(1)} %bitcast.99), kind=kCustom, calls=%fused_computation.6 | custom fusion | flops 491520 | bytes 5899200 | tf_op jit(solution)/shard_map/scatter-add | solution.py:62
  69.1 1.9 collective-permute-start.7
  71.0 5.8 %collective-permute-start.6 = (f32[12,16,128]{2,1,0:T(8,128)S(1)}, f32[12,16,128]{2,1,0:T(8,128)S(1)}, u32[]{:S(2)}, u32[]{:S(2)}) collective-permute-start(f32[12,16,128]{2,1,0:T(8,128)S(1)} %get-tuple-element.14), channel_id=1, source_target_pairs={{8,0},{16,8},{24,16},{32,24},{40,32},{48,40},{56,48},{64,56},{72,6... | collective-permute-start | bytes 294920 | tf_op jit(solution)/shard_map/ppermute | solution.py:33
  78.0 0.9 collective-permute-done.6
  79.0 5.0 %fusion.41 = (f32[16]{0:T(128)S(1)}, bf16[12,16,128]{2,1,0:T(8,128)(2,1)}, f32[12,16,128]{2,1,0:T(8,128)}) fusion(bf16[12,16,128]{2,1,0:T(8,128)(2,1)S(1)} %copy-done.2, f32[12,16,128]{2,1,0:T(8,128)S(1)} %collective-permute-done.7, f32[12,16,128]{2,1,0:T(8,128)S(1)} %collective-permute-done.6, f32[37,16,128]{2,1,0:T(8,128)S(1)} %scatter_fusion.1, ...), kind=kOutput, calls=%fused_computation.60 | convolution fusion | flops 130056176 | bytes 9394480 | tf_op jit(solution)/shard_map/mrpj,mrij->rpi/dot_general | solution.py:56
  84.0 4.2 %convolution_bitcast_fusion.1 = f32[20,12,16,128]{3,2,0,1:T(8,128)} fusion(bf16[12,16,128]{2,1,0:T(8,128)(2,1)} %get-tuple-element.23, bf16[20,12,128,128]{2,3,0,1:T(8,128)(2,1)S(1)} %bitcast.95, pred[20,12]{0,1:T(8,128)(4,1)S(1)} %broadcast_compare_fusion), kind=kOutput, calls=%fused_computation.21 | convolution fusion | flops 129761280 | bytes 9879792 | tf_op jit(solution)/shard_map/rpi,mrij->mrpj/dot_general | solution.py:60
  88.2 5.8 %collective-permute-start.9 = (bf16[12,16,128]{2,1,0:T(8,128)(2,1)}, bf16[12,16,128]{2,1,0:T(8,128)(2,1)}, u32[]{:S(2)}, u32[]{:S(2)}) collective-permute-start(bf16[12,16,128]{2,1,0:T(8,128)(2,1)} %get-tuple-element.23), channel_id=1, source_target_pairs={{8,0},{16,8},{24,16},{32,24},{40,32},{48,40},{56,48},{64,56},{72,6... | collective-permute-start | bytes 147464 | tf_op jit(solution)/shard_map/ppermute | solution.py:25
  94.0 1.9 collective-permute-start.8
  96.0 57.3 %psum.28 = f32[16]{0:T(128)} all-reduce(f32[16]{0:T(128)S(1)} %get-tuple-element.22), channel_id=1, replica_groups=mesh['clus'=32,'probe'=8] {'clus'}, use_global_device_ids=true, to_apply=%region_6.8 | all-reduce | flops 16 | bytes 128 | tf_op jit(solution)/shard_map/psum | solution.py:93
  153.3 1.8 copy.89
  155.1 9.8 %scatter_fusion.2 = f32[37,16,128]{2,1,0:T(8,128)S(1)} fusion(f32[37,16,128]{2,1,0:T(8,128)S(1)} %broadcast.78.clone.2, s32[240]{0:T(256)} %copy-done.5, f32[240,16,128]{2,1,0:T(8,128)S(1)} %bitcast.100), kind=kCustom, calls=%fused_computation.7 | custom fusion | flops 491520 | bytes 5899200 | tf_op jit(solution)/shard_map/scatter-add | solution.py:62
  165.0 1.2 multiply_divide_fusion
  166.1 1.9 collective-permute-start.11
  168.1 5.8 %collective-permute-start.10 = (f32[12,16,128]{2,1,0:T(8,128)S(1)}, f32[12,16,128]{2,1,0:T(8,128)S(1)}, u32[]{:S(2)}, u32[]{:S(2)}) collective-permute-start(f32[12,16,128]{2,1,0:T(8,128)S(1)} %get-tuple-element.12), channel_id=1, source_target_pairs={{8,0},{16,8},{24,16},{32,24},{40,32},{48,40},{56,48},{64,56},{72,6... | collective-permute-start | bytes 294920 | tf_op jit(solution)/shard_map/ppermute | solution.py:33
  174.7 1.0 gather_fusion.2
  175.7 1.2 broadcast_select_fusion.3
  176.9 5.0 %fusion.81 = (bf16[12,16,128]{2,1,0:T(8,128)(2,1)}, f32[12,16,128]{2,1,0:T(8,128)}) fusion(f32[12,16,128]{2,1,0:T(8,128)} %get-tuple-element.32, f32[12,16,128]{2,1,0:T(8,128)S(1)} %collective-permute-done.11, f32[12,16,128]{2,1,0:T(8,128)S(1)} %collective-permute-done.10, f32[37,16,128]{2,1,0:T(8,128)S(1)} %scatter_fusion.2, ...), kind=kOutput, calls=%fused_computation.114 | convolution fusion | flops 129982464 | bytes 9443568 | tf_op jit(solution)/shard_map/mrpj,mrij->rpi/dot_general | solution.py:56
  181.9 3.2 convolution_bitcast_fusion
  185.2 4.9 %collective-permute-start.13 = (bf16[12,16,128]{2,1,0:T(8,128)(2,1)}, bf16[12,16,128]{2,1,0:T(8,128)(2,1)}, u32[]{:S(2)}, u32[]{:S(2)}) collective-permute-start(bf16[12,16,128]{2,1,0:T(8,128)(2,1)} %get-tuple-element.34), channel_id=1, source_target_pairs={{8,0},{16,8},{24,16},{32,24},{40,32},{48,40},{56,48},{64,56},{72,6... | collective-permute-start | bytes 147464 | tf_op jit(solution)/shard_map/ppermute | solution.py:25
  190.1 2.1 collective-permute-start.12
  192.4 9.8 %scatter_fusion.3 = f32[37,16,128]{2,1,0:T(8,128)S(1)} fusion(f32[37,16,128]{2,1,0:T(8,128)S(1)} %broadcast.78, s32[240]{0:T(256)} %copy-done.5, f32[240,16,128]{2,1,0:T(8,128)S(1)} %bitcast.101), kind=kCustom, calls=%fused_computation.8 | custom fusion | flops 491520 | bytes 5899200 | tf_op jit(solution)/shard_map/scatter-add | solution.py:62
  202.3 1.9 collective-permute-start.15
  204.2 5.8 %collective-permute-start.14 = (f32[12,16,128]{2,1,0:T(8,128)S(1)}, f32[12,16,128]{2,1,0:T(8,128)S(1)}, u32[]{:S(2)}, u32[]{:S(2)}) collective-permute-start(f32[12,16,128]{2,1,0:T(8,128)S(1)} %get-tuple-element.10), channel_id=1, source_target_pairs={{8,0},{16,8},{24,16},{32,24},{40,32},{48,40},{56,48},{64,56},{72,6... | collective-permute-start | bytes 294920 | tf_op jit(solution)/shard_map/ppermute | solution.py:33
  210.9 1.0 gather_fusion.3
  211.9 1.0 broadcast_select_fusion.2
  212.9 7.5 %multiply_convert_fusion = (bf16[12,16,128]{2,1,0:T(8,128)(2,1)S(1)}, f32[12,128]{1,0:T(8,128)S(1)}) fusion(f32[16]{0:T(128)} %multiply_divide_fusion, bf16[12,16,128]{2,1,0:T(8,128)(2,1)} %param.9, f32[12,16,128]{2,1,0:T(8,128)S(1)} %collective-permute-done.15, f32[12,16,128]{2,1,0:T(8,128)S(1)} %collective-permute-done.14, ...), kind=kOutput, calls=%fused_computation.78 | convolution fusion | flops 130521600 | bytes 9941316 | tf_op jit(solution)/shard_map/mrpj,mrij->rpi/dot_general | solution.py:56
  220.4 5.3 %collective-permute-start.17 = (bf16[12,16,128]{2,1,0:T(8,128)(2,1)S(1)}, bf16[12,16,128]{2,1,0:T(8,128)(2,1)S(1)}, u32[]{:S(2)}, u32[]{:S(2)}) collective-permute-start(bf16[12,16,128]{2,1,0:T(8,128)(2,1)S(1)} %get-tuple-element.18), channel_id=1, source_target_pairs={{8,0},{16,8},{24,16},{32,24},{40,32},{48,40},{56,48},{64,56},{72,6... | collective-permute-start | bytes 147464 | tf_op jit(solution)/shard_map/ppermute | solution.py:25
  225.7 1.9 collective-permute-start.16
  227.6 6.9 %fusion.30 = f32[12,20,128,128]{3,2,1,0:T(8,128)} fusion(bf16[20,12,16,128]{3,2,1,0:T(8,128)(2,1)S(1)} %bitcast.103, bf16[12,16,128]{2,1,0:T(8,128)(2,1)S(1)} %get-tuple-element.18), kind=kOutput, calls=%fused_computation.33 | convolution fusion | flops 125829120 | bytes 16760832 | tf_op jit(solution)/shard_map/rpi,mrpj->mrij/dot_general | solution.py:66
  234.6 1.0 gather_fusion.4
  236.0 12.0 %fusion.73 = (f32[20,12,128]{2,0,1:T(8,128)S(1)}, f32[20,12,128]{2,0,1:T(8,128)S(1)}) fusion(f32[12,20,128,128]{3,2,1,0:T(8,128)} %fusion.30, bf16[12,16,128]{2,1,0:T(8,128)(2,1)S(1)} %copy-done.3, bf16[20,12,16,128]{3,2,1,0:T(8,128)(2,1)S(1)} %bitcast.107, bf16[20,12,128,128]{2,3,0,1:T(8,128)(2,1)} %copy.79, pred[20,12]{0,1:T(8,128)(4,1)S(1)} %copy-done.14), kind=kOutput, calls=%fused_computation.106 | convolution fusion | flops 149360640 | bytes 24871152 | tf_op jit(solution)/shard_map/rpi,mrpj->mrij/dot_general | solution.py:69
  248.4 9.3 %scatter_fusion.4 = f32[37,3,128]{2,1,0:T(4,128)S(1)} fusion(f32[37,3,128]{2,1,0:T(4,128)S(1)} %broadcast_in_dim.57, s32[240]{0:T(256)S(1)} %copy-done.6, f32[240,3,128]{2,1,0:T(4,128)S(1)} %broadcast_multiply_fusion), kind=kCustom, calls=%fused_computation.9 | custom fusion | flops 92160 | bytes 1106880 | tf_op jit(solution)/shard_map/scatter-add | solution.py:80
  257.7 1.9 collective-permute-start.19
  259.6 5.8 %collective-permute-start.18 = (f32[12,3,128]{2,1,0:T(4,128)S(1)}, f32[12,3,128]{2,1,0:T(4,128)S(1)}, u32[]{:S(2)}, u32[]{:S(2)}) collective-permute-start(f32[12,3,128]{2,1,0:T(4,128)S(1)} %get-tuple-element.20), channel_id=1, source_target_pairs={{8,0},{16,8},{24,16},{32,24},{40,32},{48,40},{56,48},{64,56},{72,6... | collective-permute-start | bytes 55304 | tf_op jit(solution)/shard_map/ppermute | solution.py:33
  265.6 1.3 collective-permute-done.18
  267.2 32.7 %all-reduce = (f32[12,128]{1,0:T(8,128)S(1)}, f32[3,384]{1,0:T(4,128)}) all-reduce(f32[12,128]{1,0:T(8,128)S(1)} %get-tuple-element.19, f32[3,384]{1,0:T(4,128)S(1)} %reshape.92), channel_id=1, replica_groups=mesh['clus'=32,'probe'=8] {'probe'}, use_global_device_ids=true, to_apply=%region_8.10 | all-reduce | flops 2688 | bytes 21504 | tf_op jit(solution)/shard_map/psum | solution.py:136
  300.6 53.6 %psum.30 = f32[]{:T(128)} all-reduce(f32[]{:T(128)} %reduce_sum.66), channel_id=1, replica_groups=mesh['clus'=32,'probe'=8] {'clus'}, use_global_device_ids=true, to_apply=%region_10.12 | all-reduce | flops 1 | bytes 8 | tf_op jit(solution)/shard_map/psum | solution.py:137
  (120 shorter events, 11.6 us)
Async XLA Ops:
  0.6 44.5 %collective-permute-start.1 = (bf16[12,16,128]{2,1,0:T(8,128)(2,1)}, bf16[12,16,128]{2,1,0:T(8,128)(2,1)S(1)}, u32[]{:S(2)}, u32[]{:S(2)}) collective-permute-start(bf16[12,16,128]{2,1,0:T(8,128)(2,1)} %param.9), channel_id=1, source_target_pairs={{8,0},{16,8},{24,16},{32,24},{40,32},{48,40},{56,48},{64,56},{72,6... | collective-permute-start | bytes 147464 | tf_op jit(solution)/shard_map/ppermute | solution.py:25
  5.3 39.9 %collective-permute-start = (bf16[12,16,128]{2,1,0:T(8,128)(2,1)}, bf16[12,16,128]{2,1,0:T(8,128)(2,1)S(1)}, u32[]{:S(2)}, u32[]{:S(2)}) collective-permute-start(bf16[12,16,128]{2,1,0:T(8,128)(2,1)} %param.9), channel_id=1, source_target_pairs={{0,8},{8,16},{16,24},{24,32},{32,40},{40,48},{48,56},{56,64},{64,7... | collective-permute-start | bytes 147464 | tf_op jit(solution)/shard_map/ppermute | solution.py:22
  7.9 76.0 %copy-start.12 = (pred[20,12]{0,1:T(8,128)(4,1)}, pred[20,12]{0,1:T(8,128)(4,1)S(1)}, u32[]{:S(2)}) copy-start(pred[20,12]{0,1:T(8,128)(4,1)S(1)} %broadcast_compare_fusion) | copy-start | bytes 724
  8.8 50.5 %copy-start.5 = (s32[240]{0:T(256)}, s32[240]{0:T(256)S(1)}, u32[]{:S(2)}) copy-start(s32[240]{0:T(256)S(1)} %reshape.135) | copy-start | bytes 2884
  8.8 10.7 %copy-start.2 = (bf16[12,16,128]{2,1,0:T(8,128)(2,1)S(1)}, bf16[12,16,128]{2,1,0:T(8,128)(2,1)}, u32[]{:S(2)}) copy-start(bf16[12,16,128]{2,1,0:T(8,128)(2,1)} %param.9) | copy-start | bytes 147460
  24.1 19.4 %copy-start.10 = (bf16[3,20,12]{1,2,0:T(8,128)(2,1)S(1)}, bf16[3,20,12]{1,2,0:T(8,128)(2,1)}, u32[]{:S(2)}) copy-start(bf16[3,20,12]{1,2,0:T(8,128)(2,1)} %param.14) | copy-start | bytes 4324
  24.1 22.3 %copy-start.17 = (f32[12,128]{1,0:T(8,128)S(1)}, f32[12,128]{1,0:T(8,128)}, u32[]{:S(2)}) copy-start(f32[12,128]{1,0:T(8,128)} %param.10) | copy-start | bytes 18436
  34.1 12.3 %collective-permute-start.3 = (f32[12,16,128]{2,1,0:T(8,128)S(1)}, f32[12,16,128]{2,1,0:T(8,128)S(1)}, u32[]{:S(2)}, u32[]{:S(2)}) collective-permute-start(f32[12,16,128]{2,1,0:T(8,128)S(1)} %get-tuple-element.17), channel_id=1, source_target_pairs={{0,8},{8,16},{16,24},{24,32},{32,40},{40,48},{48,56},{56,64},{64,7... | collective-permute-start | bytes 294920 | tf_op jit(solution)/shard_map/ppermute | solution.py:33
  36.0 10.4 %collective-permute-start.2 = (f32[12,16,128]{2,1,0:T(8,128)S(1)}, f32[12,16,128]{2,1,0:T(8,128)S(1)}, u32[]{:S(2)}, u32[]{:S(2)}) collective-permute-start(f32[12,16,128]{2,1,0:T(8,128)S(1)} %get-tuple-element.16), channel_id=1, source_target_pairs={{8,0},{16,8},{24,16},{32,24},{40,32},{48,40},{56,48},{64,56},{72,6... | collective-permute-start | bytes 294920 | tf_op jit(solution)/shard_map/ppermute | solution.py:33
  42.0 35.7 %copy-start.8 = (pred[240]{0:T(512)(128)(4,1)}, pred[240]{0:T(512)(128)(4,1)S(1)}, u32[]{:S(2)}) copy-start(pred[240]{0:T(512)(128)(4,1)S(1)} %compare_and_fusion) | copy-start | bytes 724
  43.6 33.3 %copy-start.7 = (s32[1024]{0:T(1024)}, s32[1024]{0:T(1024)S(1)}, u32[]{:S(2)}) copy-start(s32[1024]{0:T(1024)S(1)} %pad_clamp_fusion) | copy-start | bytes 12292
  46.0 5.3 %slice-start = ((s8[7864320]{0:T(1024)(128)(4,1)}), s8[4194304]{0:T(1024)(128)(4,1)S(1)}, s32[]{:S(2)}) async-start(s8[7864320]{0:T(1024)(128)(4,1)} %bitcast.92), calls=%async_computation | async-start | bytes 8388608
  46.4 5.3 %slice-start.1 = ((s8[7864320]{0:T(1024)(128)(4,1)}), s8[3670016]{0:T(1024)(128)(4,1)S(1)}, s32[]{:S(2)}) async-start(s8[7864320]{0:T(1024)(128)(4,1)} %bitcast.92), calls=%async_computation.1 | async-start | bytes 7340032
  51.3 27.6 %copy-start.4 = (bf16[12,16,128]{2,1,0:T(8,128)(2,1)}, bf16[12,16,128]{2,1,0:T(8,128)(2,1)S(1)}, u32[]{:S(2)}) copy-start(bf16[12,16,128]{2,1,0:T(8,128)(2,1)S(1)} %get-tuple-element.31) | copy-start | bytes 147460
  54.2 22.6 %collective-permute-start.5 = (bf16[12,16,128]{2,1,0:T(8,128)(2,1)S(1)}, bf16[12,16,128]{2,1,0:T(8,128)(2,1)S(1)}, u32[]{:S(2)}, u32[]{:S(2)}) collective-permute-start(bf16[12,16,128]{2,1,0:T(8,128)(2,1)S(1)} %get-tuple-element.31), channel_id=1, source_target_pairs={{8,0},{16,8},{24,16},{32,24},{40,32},{48,40},{56,48},{64,56},{72,6... | collective-permute-start | bytes 147464 | tf_op jit(solution)/shard_map/ppermute | solution.py:25
  57.1 19.6 %collective-permute-start.4 = (bf16[12,16,128]{2,1,0:T(8,128)(2,1)S(1)}, bf16[12,16,128]{2,1,0:T(8,128)(2,1)S(1)}, u32[]{:S(2)}, u32[]{:S(2)}) collective-permute-start(bf16[12,16,128]{2,1,0:T(8,128)(2,1)S(1)} %get-tuple-element.31), channel_id=1, source_target_pairs={{0,8},{8,16},{16,24},{24,32},{32,40},{40,48},{48,56},{56,64},{64,7... | collective-permute-start | bytes 147464 | tf_op jit(solution)/shard_map/ppermute | solution.py:22
  69.1 9.0 %collective-permute-start.7 = (f32[12,16,128]{2,1,0:T(8,128)S(1)}, f32[12,16,128]{2,1,0:T(8,128)S(1)}, u32[]{:S(2)}, u32[]{:S(2)}) collective-permute-start(f32[12,16,128]{2,1,0:T(8,128)S(1)} %get-tuple-element.15), channel_id=1, source_target_pairs={{0,8},{8,16},{16,24},{24,32},{32,40},{40,48},{48,56},{56,64},{64,7... | collective-permute-start | bytes 294920 | tf_op jit(solution)/shard_map/ppermute | solution.py:33
  71.0 8.0 %collective-permute-start.6 = (f32[12,16,128]{2,1,0:T(8,128)S(1)}, f32[12,16,128]{2,1,0:T(8,128)S(1)}, u32[]{:S(2)}, u32[]{:S(2)}) collective-permute-start(f32[12,16,128]{2,1,0:T(8,128)S(1)} %get-tuple-element.14), channel_id=1, source_target_pairs={{8,0},{16,8},{24,16},{32,24},{40,32},{48,40},{56,48},{64,56},{72,6... | collective-permute-start | bytes 294920 | tf_op jit(solution)/shard_map/ppermute | solution.py:33
  77.7 6.3 %slice-start.2 = ((s8[7864320]{0:T(1024)(128)(4,1)}), s8[4194304]{0:T(1024)(128)(4,1)S(1)}, s32[]{:S(2)}) async-start(s8[7864320]{0:T(1024)(128)(4,1)} %bitcast.94), calls=%async_computation.2 | async-start | bytes 8388608
  78.0 5.9 %copy-start.15 = (f32[12,16,128]{2,1,0:T(8,128)}, f32[12,16,128]{2,1,0:T(8,128)S(1)}, u32[]{:S(2)}) copy-start(f32[12,16,128]{2,1,0:T(8,128)S(1)} %collective-permute-done.7) | copy-start | bytes 294916
  78.9 5.0 %copy-start.16 = (f32[12,16,128]{2,1,0:T(8,128)}, f32[12,16,128]{2,1,0:T(8,128)S(1)}, u32[]{:S(2)}) copy-start(f32[12,16,128]{2,1,0:T(8,128)S(1)} %collective-permute-done.6) | copy-start | bytes 294916
  78.9 5.0 %slice-start.3 = ((s8[7864320]{0:T(1024)(128)(4,1)}), s8[3670016]{0:T(1024)(128)(4,1)S(1)}, s32[]{:S(2)}) async-start(s8[7864320]{0:T(1024)(128)(4,1)} %bitcast.94), calls=%async_computation.3 | async-start | bytes 7340032
  88.2 85.6 %collective-permute-start.9 = (bf16[12,16,128]{2,1,0:T(8,128)(2,1)}, bf16[12,16,128]{2,1,0:T(8,128)(2,1)}, u32[]{:S(2)}, u32[]{:S(2)}) collective-permute-start(bf16[12,16,128]{2,1,0:T(8,128)(2,1)} %get-tuple-element.23), channel_id=1, source_target_pairs={{8,0},{16,8},{24,16},{32,24},{40,32},{48,40},{56,48},{64,56},{72,6... | collective-permute-start | bytes 147464 | tf_op jit(solution)/shard_map/ppermute | solution.py:25
  94.0 79.8 %collective-permute-start.8 = (bf16[12,16,128]{2,1,0:T(8,128)(2,1)}, bf16[12,16,128]{2,1,0:T(8,128)(2,1)}, u32[]{:S(2)}, u32[]{:S(2)}) collective-permute-start(bf16[12,16,128]{2,1,0:T(8,128)(2,1)} %get-tuple-element.23), channel_id=1, source_target_pairs={{0,8},{8,16},{16,24},{24,32},{32,40},{40,48},{48,56},{56,64},{64,7... | collective-permute-start | bytes 147464 | tf_op jit(solution)/shard_map/ppermute | solution.py:22
  166.1 10.7 %collective-permute-start.11 = (f32[12,16,128]{2,1,0:T(8,128)S(1)}, f32[12,16,128]{2,1,0:T(8,128)S(1)}, u32[]{:S(2)}, u32[]{:S(2)}) collective-permute-start(f32[12,16,128]{2,1,0:T(8,128)S(1)} %get-tuple-element.13), channel_id=1, source_target_pairs={{0,8},{8,16},{16,24},{24,32},{32,40},{40,48},{48,56},{56,64},{64,7... | collective-permute-start | bytes 294920 | tf_op jit(solution)/shard_map/ppermute | solution.py:33
  168.1 8.8 %collective-permute-start.10 = (f32[12,16,128]{2,1,0:T(8,128)S(1)}, f32[12,16,128]{2,1,0:T(8,128)S(1)}, u32[]{:S(2)}, u32[]{:S(2)}) collective-permute-start(f32[12,16,128]{2,1,0:T(8,128)S(1)} %get-tuple-element.12), channel_id=1, source_target_pairs={{8,0},{16,8},{24,16},{32,24},{40,32},{48,40},{56,48},{64,56},{72,6... | collective-permute-start | bytes 294920 | tf_op jit(solution)/shard_map/ppermute | solution.py:33
  175.7 6.2 %slice-start.4 = ((s8[7864320]{0:T(1024)(128)(4,1)}), s8[4194304]{0:T(1024)(128)(4,1)S(1)}, s32[]{:S(2)}) async-start(s8[7864320]{0:T(1024)(128)(4,1)} %bitcast.96), calls=%async_computation.4 | async-start | bytes 8388608
  176.9 5.0 %slice-start.5 = ((s8[7864320]{0:T(1024)(128)(4,1)}), s8[3670016]{0:T(1024)(128)(4,1)S(1)}, s32[]{:S(2)}) async-start(s8[7864320]{0:T(1024)(128)(4,1)} %bitcast.96), calls=%async_computation.5 | async-start | bytes 7340032
  176.9 5.0 %copy-start.13 = (pred[20,12]{0,1:T(8,128)(4,1)S(1)}, pred[20,12]{0,1:T(8,128)(4,1)}, u32[]{:S(2)}) copy-start(pred[20,12]{0,1:T(8,128)(4,1)} %copy-done.12) | copy-start | bytes 724
  185.2 24.9 %collective-permute-start.13 = (bf16[12,16,128]{2,1,0:T(8,128)(2,1)}, bf16[12,16,128]{2,1,0:T(8,128)(2,1)}, u32[]{:S(2)}, u32[]{:S(2)}) collective-permute-start(bf16[12,16,128]{2,1,0:T(8,128)(2,1)} %get-tuple-element.34), channel_id=1, source_target_pairs={{8,0},{16,8},{24,16},{32,24},{40,32},{48,40},{56,48},{64,56},{72,6... | collective-permute-start | bytes 147464 | tf_op jit(solution)/shard_map/ppermute | solution.py:25
  190.1 19.9 %collective-permute-start.12 = (bf16[12,16,128]{2,1,0:T(8,128)(2,1)}, bf16[12,16,128]{2,1,0:T(8,128)(2,1)}, u32[]{:S(2)}, u32[]{:S(2)}) collective-permute-start(bf16[12,16,128]{2,1,0:T(8,128)(2,1)} %get-tuple-element.34), channel_id=1, source_target_pairs={{0,8},{8,16},{16,24},{24,32},{32,40},{40,48},{48,56},{56,64},{64,7... | collective-permute-start | bytes 147464 | tf_op jit(solution)/shard_map/ppermute | solution.py:22
  202.3 10.6 %collective-permute-start.15 = (f32[12,16,128]{2,1,0:T(8,128)S(1)}, f32[12,16,128]{2,1,0:T(8,128)S(1)}, u32[]{:S(2)}, u32[]{:S(2)}) collective-permute-start(f32[12,16,128]{2,1,0:T(8,128)S(1)} %get-tuple-element.11), channel_id=1, source_target_pairs={{0,8},{8,16},{16,24},{24,32},{32,40},{40,48},{48,56},{56,64},{64,7... | collective-permute-start | bytes 294920 | tf_op jit(solution)/shard_map/ppermute | solution.py:33
  204.2 8.7 %collective-permute-start.14 = (f32[12,16,128]{2,1,0:T(8,128)S(1)}, f32[12,16,128]{2,1,0:T(8,128)S(1)}, u32[]{:S(2)}, u32[]{:S(2)}) collective-permute-start(f32[12,16,128]{2,1,0:T(8,128)S(1)} %get-tuple-element.10), channel_id=1, source_target_pairs={{8,0},{16,8},{24,16},{32,24},{40,32},{48,40},{56,48},{64,56},{72,6... | collective-permute-start | bytes 294920 | tf_op jit(solution)/shard_map/ppermute | solution.py:33
  220.4 15.2 %copy-start.9 = (pred[240]{0:T(512)(128)(4,1)S(1)}, pred[240]{0:T(512)(128)(4,1)}, u32[]{:S(2)}) copy-start(pred[240]{0:T(512)(128)(4,1)} %copy-done.8) | copy-start | bytes 724
  220.4 15.5 %copy-start.3 = (bf16[12,16,128]{2,1,0:T(8,128)(2,1)S(1)}, bf16[12,16,128]{2,1,0:T(8,128)(2,1)}, u32[]{:S(2)}) copy-start(bf16[12,16,128]{2,1,0:T(8,128)(2,1)} %param.9) | copy-start | bytes 147460
  220.4 15.5 %copy-start.14 = (pred[20,12]{0,1:T(8,128)(4,1)S(1)}, pred[20,12]{0,1:T(8,128)(4,1)}, u32[]{:S(2)}) copy-start(pred[20,12]{0,1:T(8,128)(4,1)} %copy-done.12) | copy-start | bytes 724
  220.4 14.1 %collective-permute-start.17 = (bf16[12,16,128]{2,1,0:T(8,128)(2,1)S(1)}, bf16[12,16,128]{2,1,0:T(8,128)(2,1)S(1)}, u32[]{:S(2)}, u32[]{:S(2)}) collective-permute-start(bf16[12,16,128]{2,1,0:T(8,128)(2,1)S(1)} %get-tuple-element.18), channel_id=1, source_target_pairs={{8,0},{16,8},{24,16},{32,24},{40,32},{48,40},{56,48},{64,56},{72,6... | collective-permute-start | bytes 147464 | tf_op jit(solution)/shard_map/ppermute | solution.py:25
  225.7 8.8 %collective-permute-start.16 = (bf16[12,16,128]{2,1,0:T(8,128)(2,1)S(1)}, bf16[12,16,128]{2,1,0:T(8,128)(2,1)S(1)}, u32[]{:S(2)}, u32[]{:S(2)}) collective-permute-start(bf16[12,16,128]{2,1,0:T(8,128)(2,1)S(1)} %get-tuple-element.18), channel_id=1, source_target_pairs={{0,8},{8,16},{16,24},{24,32},{32,40},{40,48},{48,56},{56,64},{64,7... | collective-permute-start | bytes 147464 | tf_op jit(solution)/shard_map/ppermute | solution.py:22
  235.9 12.1 %copy-start = (f32[240,3]{1,0:T(8,128)S(1)}, f32[240,3]{1,0:T(8,128)}, u32[]{:S(2)}) copy-start(f32[240,3]{1,0:T(8,128)} %copy.97) | copy-start | bytes 8644
  235.9 12.4 %copy-start.6 = (s32[240]{0:T(256)S(1)}, s32[240]{0:T(256)}, u32[]{:S(2)}) copy-start(s32[240]{0:T(256)} %copy-done.5) | copy-start | bytes 2884
  235.9 29.4 %copy-start.1 = (f32[20,12,3]{0,2,1:T(4,128)S(1)}, f32[20,12,3]{0,2,1:T(4,128)}, u32[]{:S(2)}) copy-start(f32[20,12,3]{0,2,1:T(4,128)} %copy.93) | copy-start | bytes 8644
  236.0 30.9 %copy-start.18 = (s32[12,128]{1,0:T(8,128)S(1)}, s32[12,128]{1,0:T(8,128)}, u32[]{:S(2)}) copy-start(s32[12,128]{1,0:T(8,128)} %param.13) | copy-start | bytes 18436
  257.7 7.9 %collective-permute-start.19 = (f32[12,3,128]{2,1,0:T(4,128)S(1)}, f32[12,3,128]{2,1,0:T(4,128)S(1)}, u32[]{:S(2)}, u32[]{:S(2)}) collective-permute-start(f32[12,3,128]{2,1,0:T(4,128)S(1)} %get-tuple-element.21), channel_id=1, source_target_pairs={{0,8},{8,16},{16,24},{24,32},{32,40},{40,48},{48,56},{56,64},{64,7... | collective-permute-start | bytes 55304 | tf_op jit(solution)/shard_map/ppermute | solution.py:33
  259.6 7.3 %collective-permute-start.18 = (f32[12,3,128]{2,1,0:T(4,128)S(1)}, f32[12,3,128]{2,1,0:T(4,128)S(1)}, u32[]{:S(2)}, u32[]{:S(2)}) collective-permute-start(f32[12,3,128]{2,1,0:T(4,128)S(1)} %get-tuple-element.20), channel_id=1, source_target_pairs={{8,0},{16,8},{24,16},{32,24},{40,32},{48,40},{56,48},{64,56},{72,6... | collective-permute-start | bytes 55304 | tf_op jit(solution)/shard_map/ppermute | solution.py:33
  300.0 54.9 %copy-start.11 = (f32[12,128]{1,0:T(8,128)}, f32[12,128]{1,0:T(8,128)S(1)}, u32[]{:S(2)}) copy-start(f32[12,128]{1,0:T(8,128)S(1)} %get-tuple-element.6) | copy-start | bytes 18436
where the time goes:
time: 357 us; the launch traced here: 356 us
  blocking collectives  144 us (40%)
  starting transfers between devices  71.8 us (20%)
  other arithmetic  57.3 us (16%)
  matrix products  55.8 us (16%)
  local copies, waits for them, and re-layouts  21.2 us (6%)
  between operations  3.99 us (1%)
    psum x1, blocking collectives, local(): norm_sq = lax.psum(partial_sq, 'clus')  57.3 us
    psum x1, blocking collectives, local(): filling = lax.psum(jnp.sum(density), 'clus') / orbitals  53.6 us
    scatter-add x4, other arithmetic, spread_terms(): jax.ops.segment_sum(flat, target_ids.reshape(-1), num_segments=segments)  39.1 us
    ppermute x10, starting transfers between devices, passed_along(): return lax.ppermute(array, axis, pairs)  38.4 us
    psum x1, blocking collectives, local(): density, atom_force = lax.psum((density_part, atom_part), 'probe')  32.7 us
    ppermute x5, starting transfers between devices, extended(): lax.ppermute(lax.slice_in_dim(block, 0, width, axis=dim), axis, backward)  23.6 us
    dot_general x4, matrix products, direct_terms(): jnp.einsum('mrpj,mrij->rpi', picked, blocks, preferred_element_type=jnp.f...  22.3 us
    dot_general x4, matrix products, spread_terms(): jnp.einsum('rpi,mrij->mrpj', vector_rows, blocks, preferred_element_type=...  14.4 us
  transfers between devices with their start and end apart: 20, of which 2 were waited for; matrix products, arithmetic and copies ran while one was open for 22% of the time, Pallas kernels for 0%

commit v1 on v0

v1 whole, which is shorter than its diff:
```python
import functools

import jax
import jax.numpy as jnp
import numpy as np
from jax import lax
from jax.experimental import pallas as pl
from jax.experimental.pallas import tpu as pltpu
from jax.sharding import PartitionSpec as P

MESH = pl.DeviceIdType.MESH
CL = 12
SLOTS = 20
ROWS = 16
B = 128
ATOMS = 32
REACH = 12
ORDER = 4
PROBE_VECTORS = 128
DECAY = 50.0
SMEARING_TEMP = 0.1
QUAD_NODES = 64
CHIPS_Y = 4
EMPTY = CL * SLOTS
F32 = jnp.float32
BF16 = jnp.bfloat16
FAR, NEAR = 0, 1
LINK = F32


def pair_offset(side, own, other):
    if side == FAR:
        return REACH - 1 - other - own if other + own <= REACH - 1 else None
    return 3 * REACH - 1 - other - own if other + own >= REACH - 1 else None


def kernel(
    clus, probe, probes_ref, onsite_ref, hop_ref, col_ref, atom_ref, bond_ref, mu_ref, cos_ref,
    density_ref, filling_ref, forces_ref,
    kbuf, ktbuf, tab_v, bond_v, tab, bond, xs, halo, part_out, part_in, cheb, fermi, y_acc, coef,
    norm_buf, norm_in, fill_buf, fill_in, dens_out, dens_in, wf, force_acc, col_out, col_in, onehot, z_out, z_in,
    ksem, tsem, hs, hr, ps, pr, ns, nr, gs, gr, ds, dr, fs, fr, zs, zr,
):
    me = lax.axis_index("clus")
    z = lax.axis_index("probe")
    flip = me % 2
    sign = 1 - 2 * flip
    place = [flip * (CL - 1) + sign * c for c in range(CL)]
    chip = me // 2
    cx, cy = chip // CHIPS_Y, chip % CHIPS_Y
    chips_x = clus // (2 * CHIPS_Y)

    far = ((me + clus - sign) % clus, z)
    near = (me + sign, z)
    y_peers = [((cx * CHIPS_Y + (cy + q) % CHIPS_Y) * 2 + flip, z) for q in range(1, CHIPS_Y)]
    x_peers = [((((cx + q) % chips_x) * CHIPS_Y + cy) * 2 + flip, z) for q in range(1, chips_x)]
    z_peers = [(me, (z + q) % probe) for q in range(1, probe)]

    def send(src, dst, s, r, peer):
        return pltpu.make_async_remote_copy(
            src_ref=src, dst_ref=dst, send_sem=s, recv_sem=r, device_id=peer, device_id_type=MESH
        )

    loads = [
        pltpu.make_async_copy(hop_ref.at[m], kbuf.at[pl.ds(m * CL, CL)], ksem.at[m]) for m in range(SLOTS)
    ]
    for copy in loads:
        copy.start()

    barrier = pltpu.get_barrier_semaphore()
    everyone = [far, near] + y_peers + x_peers + z_peers
    for peer in everyone:
        pl.semaphore_signal(barrier, inc=1, device_id=peer, device_id_type=MESH)

    lane = lax.broadcasted_iota(jnp.int32, (SLOTS, CL), 1)
    slot = lax.broadcasted_iota(jnp.int32, (SLOTS, CL), 0)
    columns = col_ref[...]
    rel = jnp.where(columns >= 0, columns - me * CL - lane + REACH, -1)
    rel = jnp.where(rel >= 0, rel * sign + flip * (2 * REACH), -1)
    flat = slot * CL + lane
    directions = [bond_ref[x].astype(F32) for x in range(3)]
    tab_v[...] = jnp.full(tab_v.shape, EMPTY, jnp.int32)
    bond_v[...] = jnp.zeros(bond_v.shape, F32)
    for o in range(2 * REACH + 1):
        hit = rel == o
        tab_v[o : o + 1, 0:CL] = jnp.min(jnp.where(hit, flat, EMPTY), axis=0, keepdims=True)
        for x in range(3):
            bond_v[x * 32 + o : x * 32 + o + 1, 0:CL] = jnp.sum(
                jnp.where(hit, directions[x], 0.0), axis=0, keepdims=True
            )
    tables = [pltpu.make_async_copy(tab_v, tab, tsem.at[0]), pltpu.make_async_copy(bond_v, bond, tsem.at[1])]
    for copy in tables:
        copy.start()

    nacc = jnp.zeros((ROWS, B), F32)
    for c in range(CL):
        xc = probes_ref[place[c]]
        xs[0, c] = xc
        wide = xc.astype(F32)
        cheb[0, c] = wide
        cheb[1, c] = jnp.zeros((ROWS, B), F32)
        nacc = nacc + wide * wide
    norm_buf[0] = nacc

    occupation = 1.0 / (1.0 + jnp.exp((cos_ref[1:2, :] - mu_ref[0]) / SMEARING_TEMP))
    weight = lax.broadcasted_iota(jnp.int32, (8, B), 0)
    total = jnp.sum(cos_ref[...] * occupation, axis=1, keepdims=True) * (2.0 / QUAD_NODES)
    coef[...] = jnp.broadcast_to(total, (8, B)) * jnp.where(weight == 0, 0.5, 1.0)
    for c in range(CL):
        fermi[c] = cheb[0, c] * coef[0:1, :]

    pl.semaphore_wait(barrier, len(everyone))

    def halo_copy(k, side):
        return send(xs.at[k], halo.at[k, side], hs.at[k, side], hr.at[k, side], (far, near)[side])

    def part_copy(k, side):
        return send(part_out.at[k, side], part_in.at[k, side], ps.at[k, side], pr.at[k, side], (far, near)[side])

    def stage_copies(own, arrived, s, r, stage, arriving=False):
        if stage == 0:
            return [send(own.at[0], arrived.at[0], s.at[0], r.at[0], near)]
        peers, first, count, at = ((y_peers, 1, CHIPS_Y, cy), (x_peers, 1 + CHIPS_Y, chips_x, cx))[stage - 1]
        copies = []
        for q, peer in enumerate(peers):
            slot = first + ((at + count - q - 1) % count if arriving else at)
            copies.append(send(own.at[stage], arrived.at[slot], s.at[first + q], r.at[slot], peer))
        return copies

    norm_copies = functools.partial(stage_copies, norm_buf, norm_in, ns, nr)
    fill_copies = functools.partial(stage_copies, fill_buf, fill_in, gs, gr)

    def collect(copies, own, arrived, stage):
        for copy in copies(stage, True):
            copy.wait_recv()
        if stage == 0:
            own[1] = own[0] + arrived[0]
            return
        first, count, at = ((1, CHIPS_Y, cy), (1 + CHIPS_Y, chips_x, cx))[stage - 1]
        arrived[first + at] = own[stage]
        value = arrived[first]
        for q in range(1, count):
            value = value + arrived[first + q]
        own[stage + 1] = value

    halo_copy(0, FAR).start()
    halo_copy(0, NEAR).start()
    for copy in norm_copies(0):
        copy.start()

    kbuf[EMPTY] = jnp.zeros((B, B), BF16)
    ktbuf[EMPTY] = jnp.zeros((B, B), BF16)

    def turn(m, carry):
        pltpu.make_async_copy(hop_ref.at[m], kbuf.at[pl.ds(m * CL, CL)], ksem.at[m]).wait()
        for c in range(CL):
            ktbuf[m * CL + c] = kbuf[m * CL + c].T
        return carry

    lax.fori_loop(0, SLOTS, turn, 0)
    for copy in tables:
        copy.wait()
    collect(norm_copies, norm_buf, norm_in, 0)
    for copy in norm_copies(1):
        copy.start()

    def straight(o, c):
        return kbuf[tab[o, place[c]]]

    def turned(o, c):
        return ktbuf[tab[o, place[c]]]

    def product(vectors, blocks):
        return jnp.dot(
            jnp.concatenate(vectors, axis=1), jnp.concatenate(blocks, axis=0), preferred_element_type=F32
        )

    def side_direct(k, side, c):
        others = [b for b in range(CL) if pair_offset(side, c, b) is not None]
        return product(
            [halo[k, side, b] for b in others], [turned(pair_offset(side, c, b), c) for b in others]
        )

    def apply(k, carry):
        @pl.when(k >= 1)
        def _():
            halo_copy(k, FAR).start()
            halo_copy(k, NEAR).start()

        x = [xs[k, c] for c in range(CL)]
        for side in (FAR, NEAR):
            for b in range(CL):
                own = [c for c in range(CL) if pair_offset(side, c, b) is not None]
                part_out[k, side, b] = product(
                    [x[c] for c in own], [straight(pair_offset(side, c, b), c) for c in own]
                ).astype(LINK)
            part_copy(k, side).start()
        for c in range(CL):
            y_acc[c] = product(
                x + x,
                [turned(REACH + d - c, c) for d in range(CL)] + [straight(REACH + c - d, d) for d in range(CL)],
            )

        @pl.when(k == 1)
        def _():
            collect(norm_copies, norm_buf, norm_in, 1)
            for copy in norm_copies(2):
                copy.start()

        halo_copy(k, NEAR).wait_recv()
        for c in range(CL):
            y_acc[c] = y_acc[c] + side_direct(k, NEAR, c)
        halo_copy(k, FAR).wait_recv()
        for c in range(CL):
            y_acc[c] = y_acc[c] + side_direct(k, FAR, c)
        part_copy(k, NEAR).wait_recv()
        part_copy(k, FAR).wait_recv()
        alpha = jnp.where(k == 0, 1.0, 2.0)
        into = (k + 1) % 2
        for c in range(CL):
            image = y_acc[c] + part_in[k, NEAR, c].astype(F32) + part_in[k, FAR, c].astype(F32)
            image = image + onsite_ref[pl.ds(place[c], 1), :] * xs[k, c].astype(F32)
            following = alpha * image - cheb[into, c]
            cheb[into, c] = following
            fermi[c] = fermi[c] + coef[pl.ds(k + 1, 1), :] * following
            xs[k + 1, c] = following.astype(BF16)
        return carry

    lax.fori_loop(0, ORDER, apply, 0)

    collect(norm_copies, norm_buf, norm_in, 2)
    norm_sq = jnp.sum(norm_buf[3], axis=1, keepdims=True)
    scale = jnp.broadcast_to((clus * CL * B) / (norm_sq * PROBE_VECTORS), (ROWS, B))
    for c in range(CL):
        scaled = fermi[c] * scale
        fermi[c] = scaled
        xs[ORDER, c] = scaled.astype(BF16)
    halo_copy(ORDER, FAR).start()
    halo_copy(ORDER, NEAR).start()
    filled = jnp.zeros((1, B), F32)
    dens_out[...] = jnp.zeros(dens_out.shape, F32)
    for c in range(CL):
        row = jnp.sum(xs[0, c].astype(F32) * fermi[c], axis=0, keepdims=True)
        dens_out[c : c + 1, :] = row
        filled = filled + row
        wf[c] = xs[ORDER, c].astype(F32)
    fill_buf[0] = jnp.broadcast_to(filled, (8, B))

    def z_copies(src, dst, s, r, arriving=False):
        copies = []
        for q, peer in enumerate(z_peers):
            slot = (z + probe - q - 1) % probe if arriving else z
            copies.append(send(src, dst.at[slot], s.at[q], r.at[slot], peer))
        return copies

    def z_sum(src, dst, s, r):
        dst[z] = src[...]
        for copy in z_copies(src, dst, s, r, True):
            copy.wait_recv()
        value = dst[0]
        for q in range(1, probe):
            value = value + dst[q]
        return value

    for copy in fill_copies(0):
        copy.start()
    for copy in z_copies(dens_out, dens_in, ds, dr):
        copy.start()

    def sums(left, block, u, v):
        image = jnp.dot(left, block, preferred_element_type=F32)
        r = v * image[:ROWS] + u * image[ROWS:]
        return r[:8] + r[8:]

    both = [jnp.concatenate([xs[0, c], xs[ORDER, c]], axis=0) for c in range(CL)]

    def own_vectors(c):
        return xs[0, c].astype(F32), xs[ORDER, c].astype(F32)

    def add(acc, o, c, r, positive):
        out = []
        for x in range(3):
            term = bond[x * 32 + o, place[c]] * r
            out.append(acc[x] + term if positive else acc[x] - term)
        return out

    zero3 = [jnp.zeros((8, B), F32)] * 3
    for c in range(CL):
        u, v = own_vectors(c)
        acc = zero3
        for d in range(CL):
            o = REACH + d - c
            acc = add(acc, o, c, sums(both[d], turned(o, c), u, v), False)
        for d in range(CL):
            o = REACH + c - d
            acc = add(acc, o, d, sums(both[d], straight(o, d), u, v), True)
        for x in range(3):
            force_acc[c, x] = acc[x]

    collect(fill_copies, fill_buf, fill_in, 0)
    for copy in fill_copies(1):
        copy.start()

    def col_copy(side):
        return send(col_out.at[side], col_in.at[side], fs.at[side], fr.at[side], (far, near)[side])

    def halo_both(side, b):
        return jnp.concatenate([halo[0, side, b], halo[ORDER, side, b]], axis=0)

    for side in (NEAR, FAR):
        halo_copy(ORDER, side).wait_recv()
        for b in range(CL):
            u, v = halo[0, side, b].astype(F32), halo[ORDER, side, b].astype(F32)
            acc = zero3
            for c in range(CL):
                o = pair_offset(side, c, b)
                if o is not None:
                    acc = add(acc, o, c, sums(both[c], straight(o, c), u, v), True)
            for x in range(3):
                col_out[side, 3 * b + x : 3 * b + x + 1, :] = jnp.sum(acc[x], axis=0, keepdims=True)
        col_copy(side).start()
        for c in range(CL):
            u, v = own_vectors(c)
            acc = [force_acc[c, x] for x in range(3)]
            for b in range(CL):
                o = pair_offset(side, c, b)
                if o is not None:
                    acc = add(acc, o, c, sums(halo_both(side, b), turned(o, c), u, v), False)
            for x in range(3):
                force_acc[c, x] = acc[x]

    collect(fill_copies, fill_buf, fill_in, 1)
    for copy in fill_copies(2):
        copy.start()

    row = lax.broadcasted_iota(jnp.int32, (B, B), 0)
    for c in range(CL):
        owner = atom_ref[c : c + 1, :] + ATOMS * (c % 4)
        onehot[c] = (row == owner).astype(BF16)

    summed = z_sum(dens_out, dens_in, ds, dr)
    for c in range(CL):
        density_ref[pl.ds(place[c], 1), :] = summed[c : c + 1, :]

    for side in (NEAR, FAR):
        col_copy(side).wait_recv()
    for c in range(CL):
        for x in range(3):
            j = 3 * c + x
            value = jnp.sum(force_acc[c, x], axis=0, keepdims=True)
            value = value + col_in[NEAR, j : j + 1, :] + col_in[FAR, j : j + 1, :]
            force_acc[c, x] = jnp.broadcast_to(value * DECAY, (8, B))

    dims = (((1,), (1,)), ((), ()))
    z_out[...] = jnp.zeros(z_out.shape, F32)
    pick = lax.broadcasted_iota(jnp.int32, (8, B), 0)
    for quad in range(CL // 4):
        total = jnp.zeros((8, B), F32)
        for i in range(4):
            c = quad * 4 + i
            there = place[c]
            value = jnp.where(
                pick == 0, force_acc[there, 0], jnp.where(pick == 1, force_acc[there, 1], force_acc[there, 2])
            )
            high = value.astype(BF16)
            rest = value - high.astype(F32)
            middle = rest.astype(BF16)
            low = (rest - middle.astype(F32)).astype(BF16)
            for piece in (high, middle, low):
                total = total + lax.dot_general(piece, onehot[c], dims, preferred_element_type=F32)
        z_out[pl.ds(quad * 3, 3), :] = total[0:3]
    collect(fill_copies, fill_buf, fill_in, 2)
    z_out[9:10, :] = fill_buf[3, 0:1, :]
    for copy in z_copies(z_out, z_in, zs, zr):
        copy.start()
    summed = z_sum(z_out, z_in, zs, zr)
    for quad in range(CL // 4):
        forces_ref[:, quad * B : (quad + 1) * B] = summed[quad * 3 : quad * 3 + 3]
    filling_ref[0] = jnp.sum(summed[9:10, :]) / (clus * CL * B)

    def finish(k, carry):
        for side in (FAR, NEAR):
            halo_copy(k, side).wait_send()
            part_copy(k, side).wait_send()
        return carry

    lax.fori_loop(0, ORDER, finish, 0)
    for side in (FAR, NEAR):
        halo_copy(ORDER, side).wait_send()
        col_copy(side).wait_send()
    for stage in range(3):
        for copy in norm_copies(stage) + fill_copies(stage):
            copy.wait_send()
    for copy in z_copies(dens_out, dens_in, ds, dr) + z_copies(z_out, z_in, zs, zr):
        copy.wait_send()


def cosines():
    angles = np.pi * (np.arange(QUAD_NODES) + 0.5) / QUAD_NODES
    table = np.zeros((8, B), np.float32)
    for k in range(ORDER + 1):
        table[k, :QUAD_NODES] = np.cos(k * angles)
    return table


def solution(mesh):
    clus, probe = mesh.shape["clus"], mesh.shape["probe"]
    small = 1 + CHIPS_Y + clus // (2 * CHIPS_Y)
    vmem, dma = pltpu.VMEM, pltpu.SemaphoreType.DMA

    def local(probes, onsite, hopping, block_col, atom_of, bond_dir, chemical_potential):
        in_vmem = pl.BlockSpec(memory_space=pltpu.VMEM)
        in_smem = pl.BlockSpec(memory_space=pltpu.SMEM)
        in_hbm = pl.BlockSpec(memory_space=pltpu.HBM)
        return pl.pallas_call(
            functools.partial(kernel, clus, probe),
            out_shape=(
                jax.ShapeDtypeStruct((CL, B), F32),
                jax.ShapeDtypeStruct((1,), F32),
                jax.ShapeDtypeStruct((3, CL * ATOMS), F32),
            ),
            in_specs=[in_vmem, in_vmem, in_hbm, in_vmem, in_vmem, in_vmem, in_smem, in_vmem],
            out_specs=(in_vmem, in_smem, in_vmem),
            scratch_shapes=[
                vmem((EMPTY + 1, B, B), BF16),
                vmem((EMPTY + 1, B, B), BF16),
                vmem((32, B), jnp.int32),
                vmem((96, B), F32),
                pltpu.SMEM((32, B), jnp.int32),
                pltpu.SMEM((96, B), F32),
                vmem((ORDER + 1, CL, ROWS, B), BF16),
                vmem((ORDER + 1, 2, CL, ROWS, B), BF16),
                vmem((ORDER, 2, CL, ROWS, B), LINK),
                vmem((ORDER, 2, CL, ROWS, B), LINK),
                vmem((2, CL, ROWS, B), F32),
                vmem((CL, ROWS, B), F32),
                vmem((CL, ROWS, B), F32),
                vmem((8, B), F32),
                vmem((4, ROWS, B), F32),
                vmem((small, ROWS, B), F32),
                vmem((4, 8, B), F32),
                vmem((small, 8, B), F32),
                vmem((16, B), F32),
                vmem((probe, 16, B), F32),
                vmem((CL, ROWS, B), F32),
                vmem((CL, 3, 8, B), F32),
                vmem((2, 40, B), F32),
                vmem((2, 40, B), F32),
                vmem((CL, B, B), BF16),
                vmem((16, B), F32),
                vmem((probe, 16, B), F32),
                dma((SLOTS,)),
                dma((2,)),
                dma((ORDER + 1, 2)),
                dma((ORDER + 1, 2)),
                dma((ORDER, 2)),
                dma((ORDER, 2)),
                dma((small,)),
                dma((small,)),
                dma((small,)),
                dma((small,)),
                dma((probe,)),
                dma((probe,)),
                dma((2,)),
                dma((2,)),
                dma((probe,)),
                dma((probe,)),
            ],
            compiler_params=pltpu.CompilerParams(
                collective_id=0, has_side_effects=True, vmem_limit_bytes=40 * 1024 * 1024
            ),
            cost_estimate=pl.CostEstimate(flops=2_600_000_000, bytes_accessed=8_500_000, transcendentals=0),
            name="fermi_forces",
        )(probes, onsite, hopping, block_col, atom_of, bond_dir, chemical_potential, jnp.asarray(cosines()))

    return jax.shard_map(
        local,
        mesh=mesh,
        in_specs=(
            P("clus", "probe", None),
            P("clus", None),
            P(None, "clus", None, None),
            P(None, "clus"),
            P("clus", None),
            P(None, None, "clus"),
            P(),
        ),
        out_specs=(P("clus", None), P(), P(None, "clus")),
        check_vma=False,
    )
```

time: 357 us -> 65.5 us (0.18)
  blocking collectives: 144 us -> 0 us
  starting transfers between devices: 71.8 us -> 0 us
  other arithmetic: 57.3 us -> 0 us
  matrix products: 55.8 us -> 0 us
  Pallas kernels: 0 us -> 52.4 us
  local copies, waits for them, and re-layouts: 21.2 us -> 8.91 us
    psum x3 -> x0, blocking collectives: 144 us -> none  [the longest x1 57.3 us: local(): norm_sq = lax.psum(partial_sq, 'clus')]
    ppermute x20 -> x0, starting transfers between devices: 71.8 us -> none  [the longest x10 38.4 us: passed_along(): return lax.ppermute(array, axis, pairs)]
    dot_general x11 -> x0, matrix products: 55.8 us -> none  [the longest x4 22.3 us: direct_terms(): jnp.einsum('mrpj,mrij->rpi', picked, blocks, preferred_element_type=jnp.f...]
    pallas_call x0 -> x1, Pallas kernels: none -> 52.4 us  [local(): pl.pallas_call(functools.partial(kernel, clus, probe), out_shape=(jax.Sha...]
    scatter-add x5 -> x0, other arithmetic: 48.4 us -> none  [the longest x4 39.1 us: spread_terms(): jax.ops.segment_sum(flat, target_ids.reshape(-1), num_segments=segments)]
    gather x5 -> x0, local copies, waits for them, and re-layouts: 4.63 us -> none  [gather_columns(): picked = jnp.take(source, safe_ids.reshape(-1), axis=0)]
    unnamed x51 -> x14, local copies, waits for them, and re-layouts: 11.3 us -> 8.91 us
  transfers between devices with their start and end apart: 20 -> 0, of which waited for: 2 -> 0; matrix products, arithmetic and copies ran while one was open for 22% -> 0% of each run, Pallas kernels for 0% -> 0%
where the time goes in v1:
time: 65.5 us; the launch traced here: 64.3 us
  Pallas kernels  52.4 us (80%)
  local copies, waits for them, and re-layouts  8.91 us (14%)
  between operations  2.99 us (5%)
    pallas_call x1, Pallas kernels, local(): pl.pallas_call(functools.partial(kernel, clus, probe), out_shape=(jax.Sha...  52.4 us
    unnamed x14, local copies, waits for them, and re-layouts  8.91 us

profile of v1, /device:TPU:6, one launch (start us, length us, event | category | flops | bytes accessed | tf_op | source)
XLA Modules:
  0.0 64.3 jit_solution(1492139358147497556)
XLA Ops:
  1.3 0.8 %copy.11.col_ref = s32[20,12]{1,0:T(8,128)S(1)} copy(s32[20,12]{0,1:T(8,128)} %param.11) | data formatting | bytes 1920 | tf_op args[3]
  2.1 0.8 %copy.12.bond_ref = bf16[3,20,12]{2,1,0:T(8,128)(2,1)S(1)} copy(bf16[3,20,12]{1,2,0:T(8,128)(2,1)} %param.13) | data formatting | bytes 2880 | tf_op args[5]
  2.9 0.0 copy-start
  2.9 3.2 %copy-done = bf16[20,12,128,128]{3,2,1,0:T(8,128)(2,1)S(1)} copy-done((bf16[20,12,128,128]{3,2,1,0:T(8,128)(2,1)S(1)}, bf16[20,12,128,128]{3,2,1,0:T(8,128)(2,1)}, u32[]{:S(2)}) %copy-start) | copy-done | bytes 7864344
  6.1 0.0 copy-start.1
  6.1 0.8 %copy-done.1 = bf16[12,16,128]{2,1,0:T(8,128)(2,1)S(1)} copy-done((bf16[12,16,128]{2,1,0:T(8,128)(2,1)S(1)}, bf16[12,16,128]{2,1,0:T(8,128)(2,1)}, u32[]{:S(2)}) %copy-start.1) | copy-done | bytes 49176
  6.9 0.0 copy-start.2
  6.9 0.7 %copy-done.2 = f32[12,128]{1,0:T(8,128)S(1)} copy-done((f32[12,128]{1,0:T(8,128)S(1)}, f32[12,128]{1,0:T(8,128)}, u32[]{:S(2)}) %copy-start.2) | copy-done | bytes 6168
  7.6 0.0 copy-start.3
  7.6 0.7 %copy-done.3 = s32[12,128]{1,0:T(8,128)S(1)} copy-done((s32[12,128]{1,0:T(8,128)S(1)}, s32[12,128]{1,0:T(8,128)}, u32[]{:S(2)}) %copy-start.3) | copy-done | bytes 6168
  8.3 0.0 copy-start.4
  8.3 0.7 %copy-done.4 = f32[8,128]{1,0:T(8,128)S(1)} copy-done((f32[8,128]{1,0:T(8,128)S(1)}, f32[8,128]{1,0:T(8,128)}, u32[]{:S(2)}) %copy-start.4) | copy-done | bytes 4120
  9.0 52.4 %fermi_forces.1 = (f32[12,128]{1,0:T(8,128)S(1)}, f32[1]{0:T(128)}, f32[3,384]{1,0:T(4,128)S(1)}) custom-call(bf16[12,16,128]{2,1,0:T(8,128)(2,1)S(1)} %copy-done.1, f32[12,128]{1,0:T(8,128)S(1)} %copy-done.2, bf16[20,12,128,128]{3,2,1,0:T(8,128)(2,1)S(1)} %copy-done, s32[20,12]{1,0:T(8,128)S(1)} %copy.11.col_ref, s32[12,128]{1,0:T(8,128)S(1)} %copy-done.3, ...), custom_call_target="tpu_custom_call" | custom-call | flops 2600000000 | bytes 8500000 | tf_op jit(solution)/shard_map/fermi_forces/pallas_call | solution.py:415
  61.4 0.6 copy.17
  62.6 0.6 copy.19
Async XLA Ops:
  2.9 3.2 %copy-start = (bf16[20,12,128,128]{3,2,1,0:T(8,128)(2,1)S(1)}, bf16[20,12,128,128]{3,2,1,0:T(8,128)(2,1)}, u32[]{:S(2)}) copy-start(bf16[20,12,128,128]{3,2,1,0:T(8,128)(2,1)} %hop_ref.1) | copy-start | bytes 23592964
  6.1 0.8 %copy-start.1 = (bf16[12,16,128]{2,1,0:T(8,128)(2,1)S(1)}, bf16[12,16,128]{2,1,0:T(8,128)(2,1)}, u32[]{:S(2)}) copy-start(bf16[12,16,128]{2,1,0:T(8,128)(2,1)} %probes_ref.1) | copy-start | bytes 147460
  6.9 0.7 %copy-start.2 = (f32[12,128]{1,0:T(8,128)S(1)}, f32[12,128]{1,0:T(8,128)}, u32[]{:S(2)}) copy-start(f32[12,128]{1,0:T(8,128)} %onsite_ref.1) | copy-start | bytes 18436
  7.6 0.7 %copy-start.3 = (s32[12,128]{1,0:T(8,128)S(1)}, s32[12,128]{1,0:T(8,128)}, u32[]{:S(2)}) copy-start(s32[12,128]{1,0:T(8,128)} %atom_ref.1) | copy-start | bytes 18436
  8.3 0.7 %copy-start.4 = (f32[8,128]{1,0:T(8,128)S(1)}, f32[8,128]{1,0:T(8,128)}, u32[]{:S(2)}) copy-start(f32[8,128]{1,0:T(8,128)} %constant.2.clone.cos_ref) | copy-start | bytes 12292

commit v2 on v1

v2 whole, which is shorter than its diff:
```python
import functools

import jax
import jax.numpy as jnp
import numpy as np
from jax import lax
from jax.experimental import pallas as pl
from jax.experimental.pallas import tpu as pltpu
from jax.sharding import PartitionSpec as P

MESH = pl.DeviceIdType.MESH
CL = 12
SLOTS = 20
ROWS = 16
B = 128
ATOMS = 32
REACH = 12
ORDER = 4
PROBE_VECTORS = 128
DECAY = 50.0
SMEARING_TEMP = 0.1
QUAD_NODES = 64
EMPTY = CL * SLOTS
F32 = jnp.float32
BF16 = jnp.bfloat16
FAR, NEAR = 0, 1
LINK = BF16


def pair_offset(side, own, other):
    if side == FAR:
        return REACH - 1 - other - own if other + own <= REACH - 1 else None
    return 3 * REACH - 1 - other - own if other + own >= REACH - 1 else None


def kernel(
    clus, probe, probes_hbm, onsite_hbm, hop_ref, col_hbm, atom_hbm, bond_hbm, mu_hbm, cos_hbm,
    density_hbm, filling_hbm, forces_hbm,
    density_ref, filling_ref, forces_ref, mu_ref, probes_ref, onsite_ref, col_ref, atom_ref, bond_ref, cos_ref, atom_far, kbuf, ktbuf, tab_v, bond_v, tab, bond, xs, halo, part_out, part_in, cheb, fermi, y_acc, coef,
    norm_buf, norm_in, fill_buf, fill_in, dens_out, dens_in, force_acc, far_acc, col_out, col_in, onehot, z_out, z_in, f_out, f_in,
    isem, osem, ksem, tsem, asem, hs, hr, ps, pr, ns, nr, gs, gr, ds, dr, fs, fr, zs, zr, ws, wr,
):
    me = lax.axis_index("clus")
    z = lax.axis_index("probe")
    flip = me % 2
    sign = 1 - 2 * flip
    place = [flip * (CL - 1) + sign * c for c in range(CL)]
    chips = clus // 2
    chip = me // 2
    has_far = jnp.logical_and(me > 0, me < clus - 1)

    far_clus = (me + clus - sign) % clus
    far = (far_clus, z)
    near = (me + sign, z)
    chip_peers = [(((chip + q) % chips) * 2 + flip, z) for q in range(1, chips)]
    z_peers = [(me, (z + q) % probe) for q in range(1, probe)]
    far_peers = [(far_clus, (z + q) % probe) for q in range(probe)]

    barrier = pltpu.get_barrier_semaphore()
    everyone = [near] + chip_peers + z_peers
    for peer in everyone:
        pl.semaphore_signal(barrier, inc=1, device_id=peer, device_id_type=MESH)

    @pl.when(has_far)
    def _():
        for peer in far_peers:
            pl.semaphore_signal(barrier, inc=1, device_id=peer, device_id_type=MESH)

    def send(src, dst, s, r, peer):
        return pltpu.make_async_remote_copy(
            src_ref=src, dst_ref=dst, send_sem=s, recv_sem=r, device_id=peer, device_id_type=MESH
        )

    loads = [
        pltpu.make_async_copy(hop_ref.at[m], kbuf.at[pl.ds(m * CL, CL)], ksem.at[m]) for m in range(SLOTS)
    ]
    inputs = [
        pltpu.make_async_copy(source, target, isem.at[i])
        for i, (source, target) in enumerate(
            (
                (col_hbm, col_ref), (bond_hbm, bond_ref), (probes_hbm, probes_ref), (cos_hbm, cos_ref),
                (atom_hbm, atom_ref), (onsite_hbm, onsite_ref), (mu_hbm, mu_ref),
            )
        )
    ]
    for copy in inputs + loads:
        copy.start()
    for copy in inputs:
        copy.wait()

    lane = lax.broadcasted_iota(jnp.int32, (CL, SLOTS), 0)
    slot = lax.broadcasted_iota(jnp.int32, (CL, SLOTS), 1)
    columns = col_ref[...]
    rel = jnp.where(columns >= 0, columns - me * CL - lane + REACH, -1)
    rel = jnp.where(rel >= 0, rel * sign + flip * (2 * REACH), -1)
    flat = slot * CL + lane
    directions = [bond_ref[x].astype(F32) for x in range(3)]
    wide_lane = lax.broadcasted_iota(jnp.int32, (CL, B), 1)
    places = jnp.full((CL, B), EMPTY, jnp.int32)
    facing = [jnp.zeros((CL, B), F32)] * 3
    for o in range(2 * REACH + 1):
        hit = rel == o
        here = wide_lane == o
        places = jnp.where(here, jnp.min(jnp.where(hit, flat, EMPTY), axis=1, keepdims=True), places)
        for x in range(3):
            facing[x] = jnp.where(
                here, jnp.sum(jnp.where(hit, directions[x], 0.0), axis=1, keepdims=True), facing[x]
            )
    tab_v[0:CL, :] = places
    for x in range(3):
        bond_v[16 * x : 16 * x + CL, :] = facing[x]
    tables = [pltpu.make_async_copy(tab_v, tab, tsem.at[0]), pltpu.make_async_copy(bond_v, bond, tsem.at[1])]
    for copy in tables:
        copy.start()

    @pl.when(jnp.logical_not(has_far))
    def _():
        f_in[...] = jnp.zeros(f_in.shape, F32)
        atom_far[...] = jnp.zeros(atom_far.shape, jnp.int32)
        halo[:, FAR] = jnp.zeros((ORDER + 1, CL, ROWS, B), BF16)
        part_in[:, FAR] = jnp.zeros((ORDER, CL, ROWS, B), LINK)

    nacc = jnp.zeros((ROWS, B), F32)
    for c in range(CL):
        xc = probes_ref[place[c]]
        xs[0, c] = xc
        wide = xc.astype(F32)
        cheb[0, c] = wide
        cheb[1, c] = jnp.zeros((ROWS, B), F32)
        nacc = nacc + wide * wide
    norm_buf[0] = nacc

    occupation = 1.0 / (1.0 + jnp.exp((cos_ref[1:2, :] - mu_ref[0]) / SMEARING_TEMP))
    weight = lax.broadcasted_iota(jnp.int32, (8, B), 0)
    total = jnp.sum(cos_ref[...] * occupation, axis=1, keepdims=True) * (2.0 / QUAD_NODES)
    coef[...] = jnp.broadcast_to(total, (8, B)) * jnp.where(weight == 0, 0.5, 1.0)
    for c in range(CL):
        fermi[c] = cheb[0, c] * coef[0:1, :]

    pl.semaphore_wait(barrier, len(everyone) + len(far_peers) * has_far.astype(jnp.int32))

    def halo_copy(k, side):
        return send(xs.at[k], halo.at[k, side], hs.at[k, side], hr.at[k, side], (far, near)[side])

    def part_copy(k, side):
        return send(part_out.at[k, side], part_in.at[k, side], ps.at[k, side], pr.at[k, side], (far, near)[side])

    def stage_copies(own, arrived, s, r, stage, arriving=False):
        if stage == 0:
            return [send(own.at[0], arrived.at[chips], s.at[0], r.at[chips], near)]
        copies = []
        for q, peer in enumerate(chip_peers):
            place_in = (chip + chips - q - 1) % chips if arriving else chip
            copies.append(send(own.at[stage], arrived.at[place_in], s.at[1 + q], r.at[place_in], peer))
        return copies

    norm_copies = functools.partial(stage_copies, norm_buf, norm_in, ns, nr)
    fill_copies = functools.partial(stage_copies, fill_buf, fill_in, gs, gr)

    def collect(copies, own, arrived, stage):
        for copy in copies(stage, True):
            copy.wait_recv()
        if stage == 0:
            own[1] = own[0] + arrived[chips]
            return
        arrived[chip] = own[stage]
        value = arrived[0]
        for q in range(1, chips):
            value = value + arrived[q]
        own[stage + 1] = value

    def atoms_copy():
        return send(atom_ref, atom_far, asem.at[0], asem.at[1], far)

    @pl.when(has_far)
    def _():
        halo_copy(0, FAR).start()
        atoms_copy().start()

    halo_copy(0, NEAR).start()
    for copy in norm_copies(0):
        copy.start()

    kbuf[EMPTY] = jnp.zeros((B, B), BF16)
    ktbuf[EMPTY] = jnp.zeros((B, B), BF16)

    def turn(m, carry):
        pltpu.make_async_copy(hop_ref.at[m], kbuf.at[pl.ds(m * CL, CL)], ksem.at[m]).wait()
        for c in range(CL):
            ktbuf[m * CL + c] = kbuf[m * CL + c].T
        return carry

    lax.fori_loop(0, SLOTS, turn, 0)
    for copy in tables:
        copy.wait()
    collect(norm_copies, norm_buf, norm_in, 0)
    for copy in norm_copies(1):
        copy.start()

    def straight(o, c):
        return kbuf[tab[place[c], o]]

    def turned(o, c):
        return ktbuf[tab[place[c], o]]

    def product(vectors, blocks):
        return jnp.dot(
            jnp.concatenate(vectors, axis=1), jnp.concatenate(blocks, axis=0), preferred_element_type=F32
        )

    def side_direct(k, side, c):
        others = [b for b in range(CL) if pair_offset(side, c, b) is not None]
        return product(
            [halo[k, side, b] for b in others], [turned(pair_offset(side, c, b), c) for b in others]
        )

    def apply(k, carry):
        @pl.when(jnp.logical_and(k >= 1, has_far))
        def _():
            halo_copy(k, FAR).start()

        @pl.when(k >= 1)
        def _():
            halo_copy(k, NEAR).start()

        x = [xs[k, c] for c in range(CL)]
        for side in (FAR, NEAR):
            for b in range(CL):
                own = [c for c in range(CL) if pair_offset(side, c, b) is not None]
                part_out[k, side, b] = product(
                    [x[c] for c in own], [straight(pair_offset(side, c, b), c) for c in own]
                ).astype(LINK)
            if side == FAR:

                @pl.when(has_far)
                def _():
                    part_copy(k, FAR).start()

            else:
                part_copy(k, NEAR).start()
        for c in range(CL):
            y_acc[c] = product(
                x + x,
                [turned(REACH + d - c, c) for d in range(CL)] + [straight(REACH + c - d, d) for d in range(CL)],
            )

        @pl.when(k == 2)
        def _():
            collect(norm_copies, norm_buf, norm_in, 1)
            norm_sq = jnp.sum(norm_buf[2], axis=1, keepdims=True)
            norm_buf[3] = jnp.broadcast_to((clus * CL * B) / (norm_sq * PROBE_VECTORS), (ROWS, B))

        halo_copy(k, NEAR).wait_recv()
        for c in range(CL):
            y_acc[c] = y_acc[c] + side_direct(k, NEAR, c)
        part_copy(k, NEAR).wait_recv()

        @pl.when(has_far)
        def _():
            halo_copy(k, FAR).wait_recv()

        for c in range(CL):
            y_acc[c] = y_acc[c] + part_in[k, NEAR, c].astype(F32) + side_direct(k, FAR, c)

        @pl.when(has_far)
        def _():
            part_copy(k, FAR).wait_recv()

        alpha = jnp.where(k == 0, 1.0, 2.0)
        into = (k + 1) % 2
        for c in range(CL):
            image = y_acc[c] + part_in[k, FAR, c].astype(F32)
            image = image + onsite_ref[pl.ds(place[c], 1), :] * xs[k, c].astype(F32)
            following = alpha * image - cheb[into, c]
            cheb[into, c] = following
            fermi[c] = fermi[c] + coef[pl.ds(k + 1, 1), :] * following
            xs[k + 1, c] = following.astype(BF16)
        return carry

    lax.fori_loop(0, ORDER, apply, 0)

    scale = norm_buf[3]
    for c in range(CL):
        scaled = fermi[c] * scale
        fermi[c] = scaled
        xs[ORDER, c] = scaled.astype(BF16)

    @pl.when(has_far)
    def _():
        halo_copy(ORDER, FAR).start()

    halo_copy(ORDER, NEAR).start()
    filled = jnp.zeros((1, B), F32)
    dens_out[...] = jnp.zeros(dens_out.shape, F32)
    for c in range(CL):
        row = jnp.sum(xs[0, c].astype(F32) * fermi[c], axis=0, keepdims=True)
        dens_out[c : c + 1, :] = row
        filled = filled + row
    fill_buf[0] = jnp.broadcast_to(filled, (8, B))

    def z_copies(src, dst, s, r, arriving=False):
        copies = []
        for q, peer in enumerate(z_peers):
            slot = (z + probe - q - 1) % probe if arriving else z
            copies.append(send(src, dst.at[slot], s.at[q], r.at[slot], peer))
        return copies

    def z_sum(src, dst, s, r):
        dst[z] = src[...]
        for copy in z_copies(src, dst, s, r, True):
            copy.wait_recv()
        value = dst[0]
        for q in range(1, probe):
            value = value + dst[q]
        return value

    for copy in fill_copies(0):
        copy.start()
    for copy in z_copies(dens_out, dens_in, ds, dr):
        copy.start()

    def sums(left, block, u, v):
        image = jnp.dot(left, block, preferred_element_type=F32)
        r = v * image[:ROWS] + u * image[ROWS:]
        return r[:8] + r[8:]

    both = [jnp.concatenate([xs[0, c], xs[ORDER, c]], axis=0) for c in range(CL)]

    def own_vectors(c):
        return xs[0, c].astype(F32), xs[ORDER, c].astype(F32)

    def add(acc, o, c, r, positive):
        out = []
        for x in range(3):
            term = bond[16 * x + place[c], o] * r
            out.append(acc[x] + term if positive else acc[x] - term)
        return out

    zero3 = [jnp.zeros((8, B), F32)] * 3
    for c in range(CL):
        if c == CL // 3:
            collect(fill_copies, fill_buf, fill_in, 0)
            for copy in fill_copies(1):
                copy.start()
        u, v = own_vectors(c)
        acc = zero3
        for d in range(CL):
            o = REACH + d - c
            acc = add(acc, o, c, sums(both[d], turned(o, c), u, v), False)
        for d in range(CL):
            o = REACH + c - d
            acc = add(acc, o, d, sums(both[d], straight(o, d), u, v), True)
        for x in range(3):
            force_acc[c, x] = acc[x]

    def col_copy():
        return send(col_out, col_in, fs.at[0], fr.at[0], near)

    row = lax.broadcasted_iota(jnp.int32, (B, B), 0)

    @pl.when(has_far)
    def _():
        atoms_copy().wait_recv()

    for c in range(CL):
        onehot[0, c] = (row == atom_ref[c : c + 1, :] + ATOMS * (c % 4)).astype(BF16)
        onehot[1, c] = (row == atom_far[c : c + 1, :] + ATOMS * (c % 4)).astype(BF16)

    dims = (((1,), (1,)), ((), ()))
    pick = lax.broadcasted_iota(jnp.int32, (8, B), 0)

    def atom_sums(which, source, target):
        for quad in range(CL // 4):
            total = jnp.zeros((8, B), F32)
            for c in range(quad * 4, quad * 4 + 4):
                value = jnp.where(pick == 0, source(c, 0), jnp.where(pick == 1, source(c, 1), source(c, 2)))
                high = value.astype(BF16)
                rest = value - high.astype(F32)
                middle = rest.astype(BF16)
                low = (rest - middle.astype(F32)).astype(BF16)
                for piece in (high, middle, low):
                    total = total + lax.dot_general(piece, onehot[which, c], dims, preferred_element_type=F32)
            target[quad * 3 : quad * 3 + 3, :] = total[0:3]

    def far_copies(arriving=False):
        copies = []
        for q, peer in enumerate(far_peers):
            place_in = (z + probe - q) % probe if arriving else z
            copies.append(send(f_out, f_in.at[place_in], ws.at[q], wr.at[place_in], peer))
        return copies

    def halo_both(side, b):
        return jnp.concatenate([halo[0, side, b], halo[ORDER, side, b]], axis=0)

    z_out[...] = jnp.zeros(z_out.shape, F32)
    f_out[...] = jnp.zeros(f_out.shape, F32)
    for side in (NEAR, FAR):
        if side == NEAR:
            halo_copy(ORDER, NEAR).wait_recv()
        else:

            @pl.when(has_far)
            def _():
                halo_copy(ORDER, FAR).wait_recv()

        for b in range(CL):
            u, v = halo[0, side, b].astype(F32), halo[ORDER, side, b].astype(F32)
            acc = zero3
            for c in range(CL):
                o = pair_offset(side, c, b)
                if o is not None:
                    acc = add(acc, o, c, sums(both[c], straight(o, c), u, v), True)
            for x in range(3):
                total = jnp.sum(acc[x], axis=0, keepdims=True)
                if side == NEAR:
                    col_out[3 * b + x : 3 * b + x + 1, :] = total
                else:
                    far_acc[b, x] = jnp.broadcast_to(total * DECAY, (8, B))
        if side == NEAR:
            col_copy().start()
        else:
            atom_sums(1, lambda c, x: far_acc[(1 - flip) * (CL - 1) - sign * c, x], f_out)

            @pl.when(has_far)
            def _():
                for copy in far_copies():
                    copy.start()

        for c in range(CL):
            u, v = own_vectors(c)
            acc = [force_acc[c, x] for x in range(3)]
            for b in range(CL):
                o = pair_offset(side, c, b)
                if o is not None:
                    acc = add(acc, o, c, sums(halo_both(side, b), turned(o, c), u, v), False)
            for x in range(3):
                force_acc[c, x] = acc[x]

    col_copy().wait_recv()
    for c in range(CL):
        for x in range(3):
            j = 3 * c + x
            value = jnp.sum(force_acc[c, x], axis=0, keepdims=True) + col_in[j : j + 1, :]
            force_acc[c, x] = jnp.broadcast_to(value * DECAY, (8, B))
    atom_sums(0, lambda c, x: force_acc[place[c], x], z_out)
    collect(fill_copies, fill_buf, fill_in, 1)
    z_out[9:10, :] = fill_buf[2, 0:1, :]
    for copy in z_copies(z_out, z_in, zs, zr):
        copy.start()

    summed = z_sum(dens_out, dens_in, ds, dr)
    for c in range(CL):
        density_ref[pl.ds(place[c], 1), :] = summed[c : c + 1, :]
    results = [
        pltpu.make_async_copy(source, target, osem.at[i])
        for i, (source, target) in enumerate(
            ((density_ref, density_hbm), (forces_ref, forces_hbm), (filling_ref, filling_hbm))
        )
    ]
    results[0].start()

    @pl.when(has_far)
    def _():
        for copy in far_copies(True):
            copy.wait_recv()

    summed = z_sum(z_out, z_in, zs, zr)
    for q in range(probe):
        summed = summed + f_in[q]
    for quad in range(CL // 4):
        forces_ref[:, quad * B : (quad + 1) * B] = summed[quad * 3 : quad * 3 + 3]
    results[1].start()
    filling_ref[0] = jnp.sum(summed[9:10, :]) / (clus * CL * B)
    results[2].start()

    def finish(k, carry):
        halo_copy(k, NEAR).wait_send()
        part_copy(k, NEAR).wait_send()

        @pl.when(has_far)
        def _():
            halo_copy(k, FAR).wait_send()
            part_copy(k, FAR).wait_send()

        return carry

    lax.fori_loop(0, ORDER, finish, 0)
    halo_copy(ORDER, NEAR).wait_send()
    col_copy().wait_send()

    @pl.when(has_far)
    def _():
        halo_copy(ORDER, FAR).wait_send()
        atoms_copy().wait_send()
        for copy in far_copies():
            copy.wait_send()

    for stage in range(2):
        for copy in norm_copies(stage) + fill_copies(stage):
            copy.wait_send()
    for copy in z_copies(dens_out, dens_in, ds, dr) + z_copies(z_out, z_in, zs, zr):
        copy.wait_send()
    for copy in results:
        copy.wait()


def hand_over(density, filling, forces, density_out, filling_out, forces_out, sems):
    copies = [
        pltpu.make_async_copy(source, target, sems.at[i])
        for i, (source, target) in enumerate(((density, density_out), (filling, filling_out), (forces, forces_out)))
    ]
    for copy in copies:
        copy.start()
    for copy in copies:
        copy.wait()


def cosines():
    angles = np.pi * (np.arange(QUAD_NODES) + 0.5) / QUAD_NODES
    table = np.zeros((8, B), np.float32)
    for k in range(ORDER + 1):
        table[k, :QUAD_NODES] = np.cos(k * angles)
    return table


def solution(mesh):
    clus, probe = mesh.shape["clus"], mesh.shape["probe"]
    small = 1 + clus // 2
    vmem, dma = pltpu.VMEM, pltpu.SemaphoreType.DMA

    def local(probes, onsite, hopping, block_col, atom_of, bond_dir, chemical_potential):
        in_hbm = pl.BlockSpec(memory_space=pltpu.HBM)
        shapes = (
            jax.ShapeDtypeStruct((CL, B), F32),
            jax.ShapeDtypeStruct((1,), F32),
            jax.ShapeDtypeStruct((3, CL * ATOMS), F32),
        )
        found = pl.pallas_call(
            functools.partial(kernel, clus, probe),
            out_shape=shapes,
            in_specs=[in_hbm] * 8,
            out_specs=(in_hbm,) * 3,
            scratch_shapes=[
                vmem((CL, B), F32),
                pltpu.SMEM((1,), F32),
                vmem((3, CL * ATOMS), F32),
                pltpu.SMEM((1,), F32),
                vmem((CL, ROWS, B), BF16),
                vmem((CL, B), F32),
                vmem((CL, SLOTS), jnp.int32),
                vmem((CL, B), jnp.int32),
                vmem((3, CL, SLOTS), BF16),
                vmem((8, B), F32),
                vmem((CL, B), jnp.int32),
                vmem((EMPTY + 1, B, B), BF16),
                vmem((EMPTY + 1, B, B), BF16),
                vmem((16, B), jnp.int32),
                vmem((48, B), F32),
                pltpu.SMEM((16, B), jnp.int32),
                pltpu.SMEM((48, B), F32),
                vmem((ORDER + 1, CL, ROWS, B), BF16),
                vmem((ORDER + 1, 2, CL, ROWS, B), BF16),
                vmem((ORDER, 2, CL, ROWS, B), LINK),
                vmem((ORDER, 2, CL, ROWS, B), LINK),
                vmem((2, CL, ROWS, B), F32),
                vmem((CL, ROWS, B), F32),
                vmem((CL, ROWS, B), F32),
                vmem((8, B), F32),
                vmem((4, ROWS, B), F32),
                vmem((small, ROWS, B), F32),
                vmem((4, 8, B), F32),
                vmem((small, 8, B), F32),
                vmem((16, B), F32),
                vmem((probe, 16, B), F32),
                vmem((CL, 3, 8, B), F32),
                vmem((CL, 3, 8, B), F32),
                vmem((40, B), F32),
                vmem((40, B), F32),
                vmem((2, CL, B, B), BF16),
                vmem((16, B), F32),
                vmem((probe, 16, B), F32),
                vmem((16, B), F32),
                vmem((probe, 16, B), F32),
                dma((7,)),
                dma((3,)),
                dma((SLOTS,)),
                dma((2,)),
                dma((2,)),
                dma((ORDER + 1, 2)),
                dma((ORDER + 1, 2)),
                dma((ORDER, 2)),
                dma((ORDER, 2)),
                dma((small,)),
                dma((small,)),
                dma((small,)),
                dma((small,)),
                dma((probe,)),
                dma((probe,)),
                dma((1,)),
                dma((1,)),
                dma((probe,)),
                dma((probe,)),
                dma((probe,)),
                dma((probe,)),
            ],
            compiler_params=pltpu.CompilerParams(
                collective_id=0, has_side_effects=True, vmem_limit_bytes=60 * 1024 * 1024
            ),
            cost_estimate=pl.CostEstimate(flops=2_600_000_000, bytes_accessed=8_500_000, transcendentals=0),
            name="fermi_forces",
        )(
            probes, onsite, hopping, block_col.T, atom_of, jnp.swapaxes(bond_dir, 1, 2), chemical_potential,
            jnp.asarray(cosines()),
        )
        return pl.pallas_call(
            hand_over,
            out_shape=shapes,
            in_specs=[in_hbm] * 3,
            out_specs=(in_hbm,) * 3,
            scratch_shapes=[dma((3,))],
            compiler_params=pltpu.CompilerParams(vmem_limit_bytes=60 * 1024 * 1024),
            name="hand_over",
        )(*found)

    return jax.shard_map(
        local,
        mesh=mesh,
        in_specs=(
            P("clus", "probe", None),
            P("clus", None),
            P(None, "clus", None, None),
            P(None, "clus"),
            P("clus", None),
            P(None, None, "clus"),
            P(),
        ),
        out_specs=(P("clus", None), P(), P(None, "clus")),
        check_vma=False,
    )
```

time: 65.5 us -> 49.2 us (0.75); the launches traced: 64.3 us -> 48.7 us
  local copies, waits for them, and re-layouts: 8.91 us -> 0 us
  Pallas kernels: 52.4 us -> 47.5 us
  between operations: 2.99 us -> 1.29 us
    unnamed x14 -> x0, local copies, waits for them, and re-layouts: 8.91 us -> none
    pallas_call x1 -> x2, Pallas kernels: 52.4 us -> 47.5 us  [the longest x1 45.3 us: local(): pl.pallas_call(functools.partial(kernel, clus, probe), out_shape=shapes,...]
where the time goes in v2:
time: 49.2 us; the launch traced here: 48.7 us
  Pallas kernels  47.5 us (97%)
  between operations  1.29 us (3%)
    pallas_call x1, Pallas kernels, local(): pl.pallas_call(functools.partial(kernel, clus, probe), out_shape=shapes,...  45.3 us
    pallas_call x1, Pallas kernels, local(): pl.pallas_call(hand_over, out_shape=shapes, in_specs=[in_hbm] * 3, out_sp...  2.13 us

profile of v2, /device:TPU:6, one launch (start us, length us, event | category | flops | bytes accessed | tf_op | source)
XLA Modules:
  0.0 48.7 jit_solution(3641837237040939156)
XLA Ops:
  1.3 45.3 %fermi_forces.1 = (f32[12,128]{1,0:T(8,128)}, f32[1]{0:T(128)}, f32[3,384]{1,0:T(4,128)}) custom-call(bf16[12,16,128]{2,1,0:T(8,128)(2,1)} %probes_hbm.1, f32[12,128]{1,0:T(8,128)} %onsite_hbm.1, bf16[20,12,128,128]{3,2,1,0:T(8,128)(2,1)} %hop_ref.1, s32[12,20]{1,0:T(8,128)} %bitcast.3, s32[12,128]{1,0:T(8,128)} %atom_hbm.1, bf16[3,12,20]{2,1,0:T(8,128)(2,1)} %bitcast.2, ...), custom_call_target="tpu_custom_call" | custom-call | flops 2600000000 | bytes 8500000 | tf_op jit(solution)/shard_map/fermi_forces/pallas_call | solution.py:538
  46.6 2.1 %hand_over.1 = (f32[12,128]{1,0:T(8,128)}, f32[1]{0:T(128)}, f32[3,384]{1,0:T(4,128)}) custom-call(f32[12,128]{1,0:T(8,128)} %get-tuple-element.6.density, f32[1]{0:T(128)} %get-tuple-element.7.filling, f32[3,384]{1,0:T(4,128)} %get-tuple-element.8.forces), custom_call_target="tpu_custom_call" | custom-call | tf_op jit(solution)/shard_map/hand_over/pallas_call | solution.py:615

commit v3 on v2

--- a/solution.py
+++ b/solution.py
@@ -13,6 +13,7 @@
 SLOTS = 20
 ROWS = 16
 B = 128
+CHIPS_Y = 4
 ATOMS = 32
 REACH = 12
 ORDER = 4
@@ -37,8 +38,8 @@
     clus, probe, probes_hbm, onsite_hbm, hop_ref, col_hbm, atom_hbm, bond_hbm, mu_hbm, cos_hbm,
     density_hbm, filling_hbm, forces_hbm,
     density_ref, filling_ref, forces_ref, mu_ref, probes_ref, onsite_ref, col_ref, atom_ref, bond_ref, cos_ref, atom_far, kbuf, ktbuf, tab_v, bond_v, tab, bond, xs, halo, part_out, part_in, cheb, fermi, y_acc, coef,
-    norm_buf, norm_in, fill_buf, fill_in, dens_out, dens_in, force_acc, far_acc, col_out, col_in, onehot, z_out, z_in, f_out, f_in,
-    isem, osem, ksem, tsem, asem, hs, hr, ps, pr, ns, nr, gs, gr, ds, dr, fs, fr, zs, zr, ws, wr,
+    norm_buf, norm_in, fill_buf, fill_in, dens_out, dens_in, force_acc, far_acc, ahead, col_out, col_in, onehot, z_out, z_in, f_out, f_in,
+    isem, osem, ksem, tsem, asem, hs, hr, ps, pr, ns, nr, gs, gr, ds, dr, fs, fr, zs, zr, ws, wr, word,
 ):
     me = lax.axis_index("clus")
     z = lax.axis_index("probe")
@@ -56,15 +57,28 @@
     z_peers = [(me, (z + q) % probe) for q in range(1, probe)]
     far_peers = [(far_clus, (z + q) % probe) for q in range(probe)]
 
+    chips_x = chips // CHIPS_Y
+    cx, cy = chip // CHIPS_Y, chip % CHIPS_Y
+    along_x = [((((cx + q) % chips_x) * CHIPS_Y + cy) * 2 + flip, z) for q in (1, chips_x - 1)]
+    along_y = [((cx * CHIPS_Y + (cy + q) % CHIPS_Y) * 2 + flip, z) for q in (1, CHIPS_Y - 1)]
+    along_z = [(me, (z + q) % probe) for q in (1, probe - 1)]
+    rounds = [along_z + along_y, along_z + along_y, along_z + along_x, along_z + along_x]
+
+    def spread(i):
+        for peer in rounds[i]:
+            pl.semaphore_signal(word.at[i], inc=1, device_id=peer, device_id_type=MESH)
+
+    def heard(i):
+        pl.semaphore_wait(word.at[i], len(rounds[i]))
+
     barrier = pltpu.get_barrier_semaphore()
-    everyone = [near] + chip_peers + z_peers
+    everyone = [near] + along_x + along_y + along_z
     for peer in everyone:
         pl.semaphore_signal(barrier, inc=1, device_id=peer, device_id_type=MESH)
 
     @pl.when(has_far)
     def _():
-        for peer in far_peers:
-            pl.semaphore_signal(barrier, inc=1, device_id=peer, device_id_type=MESH)
+        pl.semaphore_signal(barrier, inc=1, device_id=far, device_id_type=MESH)
 
     def send(src, dst, s, r, peer):
         return pltpu.make_async_remote_copy(
@@ -137,7 +151,7 @@
     for c in range(CL):
         fermi[c] = cheb[0, c] * coef[0:1, :]
 
-    pl.semaphore_wait(barrier, len(everyone) + len(far_peers) * has_far.astype(jnp.int32))
+    pl.semaphore_wait(barrier, len(everyone) + has_far.astype(jnp.int32))
 
     def halo_copy(k, side):
         return send(xs.at[k], halo.at[k, side], hs.at[k, side], hr.at[k, side], (far, near)[side])
@@ -155,7 +169,14 @@
         return copies
 
     norm_copies = functools.partial(stage_copies, norm_buf, norm_in, ns, nr)
-    fill_copies = functools.partial(stage_copies, fill_buf, fill_in, gs, gr)
+
+    def fill_copies(arriving=False):
+        copies = []
+        for q in range(1, clus):
+            place_in = (me + clus - q) % clus if arriving else me
+            copies.append(send(fill_buf, fill_in.at[place_in], gs.at[q], gr.at[place_in], ((me + q) % clus, z)))
+        return copies
+
 
     def collect(copies, own, arrived, stage):
         for copy in copies(stage, True):
@@ -180,22 +201,13 @@
     halo_copy(0, NEAR).start()
     for copy in norm_copies(0):
         copy.start()
+    spread(0)
 
     kbuf[EMPTY] = jnp.zeros((B, B), BF16)
     ktbuf[EMPTY] = jnp.zeros((B, B), BF16)
 
-    def turn(m, carry):
-        pltpu.make_async_copy(hop_ref.at[m], kbuf.at[pl.ds(m * CL, CL)], ksem.at[m]).wait()
-        for c in range(CL):
-            ktbuf[m * CL + c] = kbuf[m * CL + c].T
-        return carry
-
-    lax.fori_loop(0, SLOTS, turn, 0)
-    for copy in tables:
+    for copy in loads + tables:
         copy.wait()
-    collect(norm_copies, norm_buf, norm_in, 0)
-    for copy in norm_copies(1):
-        copy.start()
 
     def straight(o, c):
         return kbuf[tab[place[c], o]]
@@ -214,15 +226,7 @@
             [halo[k, side, b] for b in others], [turned(pair_offset(side, c, b), c) for b in others]
         )
 
-    def apply(k, carry):
-        @pl.when(jnp.logical_and(k >= 1, has_far))
-        def _():
-            halo_copy(k, FAR).start()
-
-        @pl.when(k >= 1)
-        def _():
-            halo_copy(k, NEAR).start()
-
+    def partials(k):
         x = [xs[k, c] for c in range(CL)]
         for side in (FAR, NEAR):
             for b in range(CL):
@@ -238,17 +242,57 @@
 
             else:
                 part_copy(k, NEAR).start()
+
+    partials(0)
+
+    def turn(m, carry):
+        for c in range(CL):
+            ktbuf[m * CL + c] = kbuf[m * CL + c].T
+        return carry
+
+    lax.fori_loop(0, SLOTS, turn, 0)
+    collect(norm_copies, norm_buf, norm_in, 0)
+
+    def apply(k, carry):
+        @pl.when(jnp.logical_and(k >= 1, has_far))
+        def _():
+            halo_copy(k, FAR).start()
+
+        @pl.when(k >= 1)
+        def _():
+            halo_copy(k, NEAR).start()
+
+        @pl.when(k >= 1)
+        def _():
+            partials(k)
+
+        x = [xs[k, c] for c in range(CL)]
         for c in range(CL):
             y_acc[c] = product(
                 x + x,
                 [turned(REACH + d - c, c) for d in range(CL)] + [straight(REACH + c - d, d) for d in range(CL)],
             )
 
+        @pl.when(k == 0)
+        def _():
+            heard(0)
+            spread(1)
+
+        @pl.when(k == 1)
+        def _():
+            heard(1)
+            spread(2)
+
         @pl.when(k == 2)
         def _():
-            collect(norm_copies, norm_buf, norm_in, 1)
-            norm_sq = jnp.sum(norm_buf[2], axis=1, keepdims=True)
-            norm_buf[3] = jnp.broadcast_to((clus * CL * B) / (norm_sq * PROBE_VECTORS), (ROWS, B))
+            heard(2)
+            spread(3)
+            for copy in norm_copies(1):
+                copy.start()
+
+        @pl.when(k == 3)
+        def _():
+            heard(3)
 
         halo_copy(k, NEAR).wait_recv()
         for c in range(CL):
@@ -279,7 +323,9 @@
 
     lax.fori_loop(0, ORDER, apply, 0)
 
-    scale = norm_buf[3]
+    collect(norm_copies, norm_buf, norm_in, 1)
+    norm_sq = jnp.sum(norm_buf[2], axis=1, keepdims=True)
+    scale = jnp.broadcast_to((clus * CL * B) / (norm_sq * PROBE_VECTORS), (ROWS, B))
     for c in range(CL):
         scaled = fermi[c] * scale
         fermi[c] = scaled
@@ -290,13 +336,10 @@
         halo_copy(ORDER, FAR).start()
 
     halo_copy(ORDER, NEAR).start()
-    filled = jnp.zeros((1, B), F32)
     dens_out[...] = jnp.zeros(dens_out.shape, F32)
     for c in range(CL):
         row = jnp.sum(xs[0, c].astype(F32) * fermi[c], axis=0, keepdims=True)
         dens_out[c : c + 1, :] = row
-        filled = filled + row
-    fill_buf[0] = jnp.broadcast_to(filled, (8, B))
 
     def z_copies(src, dst, s, r, arriving=False):
         copies = []
@@ -314,10 +357,10 @@
             value = value + dst[q]
         return value
 
-    for copy in fill_copies(0):
-        copy.start()
     for copy in z_copies(dens_out, dens_in, ds, dr):
         copy.start()
+
+    far_pairs = [(c, b) for b in range(CL) for c in range(CL) if pair_offset(FAR, c, b) is not None]
 
     def sums(left, block, u, v):
         image = jnp.dot(left, block, preferred_element_type=F32)
@@ -338,10 +381,6 @@
 
     zero3 = [jnp.zeros((8, B), F32)] * 3
     for c in range(CL):
-        if c == CL // 3:
-            collect(fill_copies, fill_buf, fill_in, 0)
-            for copy in fill_copies(1):
-                copy.start()
         u, v = own_vectors(c)
         acc = zero3
         for d in range(CL):
@@ -371,15 +410,16 @@
 
     def atom_sums(which, source, target):
         for quad in range(CL // 4):
-            total = jnp.zeros((8, B), F32)
+            pieces = []
             for c in range(quad * 4, quad * 4 + 4):
                 value = jnp.where(pick == 0, source(c, 0), jnp.where(pick == 1, source(c, 1), source(c, 2)))
-                high = value.astype(BF16)
-                rest = value - high.astype(F32)
-                middle = rest.astype(BF16)
-                low = (rest - middle.astype(F32)).astype(BF16)
-                for piece in (high, middle, low):
-                    total = total + lax.dot_general(piece, onehot[which, c], dims, preferred_element_type=F32)
+                high = value.astype(BF16).astype(F32)
+                rest = value - high
+                middle = rest.astype(BF16).astype(F32)
+                pieces.append(jnp.concatenate([high, middle, rest - middle, jnp.zeros((8, B), F32)], axis=0).astype(BF16))
+            owners = jnp.concatenate([onehot[which, c] for c in range(quad * 4, quad * 4 + 4)], axis=1)
+            total = lax.dot_general(jnp.concatenate(pieces, axis=1), owners, dims, preferred_element_type=F32)
+            total = total[0:8] + total[8:16] + total[16:24]
             target[quad * 3 : quad * 3 + 3, :] = total[0:3]
 
     def far_copies(arriving=False):
@@ -398,6 +438,8 @@
         if side == NEAR:
             halo_copy(ORDER, NEAR).wait_recv()
         else:
+            for i, (c, b) in enumerate(far_pairs):
+                ahead[i] = jnp.dot(both[c], straight(pair_offset(FAR, c, b), c), preferred_element_type=F32)
 
             @pl.when(has_far)
             def _():
@@ -408,8 +450,12 @@
             acc = zero3
             for c in range(CL):
                 o = pair_offset(side, c, b)
-                if o is not None:
+                if o is not None and side == NEAR:
                     acc = add(acc, o, c, sums(both[c], straight(o, c), u, v), True)
+                elif o is not None:
+                    image = ahead[far_pairs.index((c, b))]
+                    r = v * image[:ROWS] + u * image[ROWS:]
+                    acc = add(acc, o, c, r[:8] + r[8:], True)
             for x in range(3):
                 total = jnp.sum(acc[x], axis=0, keepdims=True)
                 if side == NEAR:
@@ -443,8 +489,6 @@
             value = jnp.sum(force_acc[c, x], axis=0, keepdims=True) + col_in[j : j + 1, :]
             force_acc[c, x] = jnp.broadcast_to(value * DECAY, (8, B))
     atom_sums(0, lambda c, x: force_acc[place[c], x], z_out)
-    collect(fill_copies, fill_buf, fill_in, 1)
-    z_out[9:10, :] = fill_buf[2, 0:1, :]
     for copy in z_copies(z_out, z_in, zs, zr):
         copy.start()
 
@@ -458,6 +502,10 @@
         )
     ]
     results[0].start()
+    fill_buf[...] = summed[0:8] + summed[8:16]
+    for copy in fill_copies():
+        copy.start()
+    fill_in[me] = fill_buf[...]
 
     @pl.when(has_far)
     def _():
@@ -470,7 +518,12 @@
     for quad in range(CL // 4):
         forces_ref[:, quad * B : (quad + 1) * B] = summed[quad * 3 : quad * 3 + 3]
     results[1].start()
-    filling_ref[0] = jnp.sum(summed[9:10, :]) / (clus * CL * B)
+    for copy in fill_copies(True):
+        copy.wait_recv()
+    filled = fill_in[0]
+    for q in range(1, clus):
+        filled = filled + fill_in[q]
+    filling_ref[0] = jnp.sum(filled) / (clus * CL * B)
     results[2].start()
 
     def finish(k, carry):
@@ -496,8 +549,10 @@
             copy.wait_send()
 
     for stage in range(2):
-        for copy in norm_copies(stage) + fill_copies(stage):
+        for copy in norm_copies(stage):
             copy.wait_send()
+    for copy in fill_copies():
+        copy.wait_send()
     for copy in z_copies(dens_out, dens_in, ds, dr) + z_copies(z_out, z_in, zs, zr):
         copy.wait_send()
     for copy in results:
@@ -566,14 +621,15 @@
                 vmem((CL, ROWS, B), F32),
                 vmem((CL, ROWS, B), F32),
                 vmem((8, B), F32),
-                vmem((4, ROWS, B), F32),
+                vmem((3, ROWS, B), F32),
                 vmem((small, ROWS, B), F32),
-                vmem((4, 8, B), F32),
-                vmem((small, 8, B), F32),
+                vmem((8, B), F32),
+                vmem((clus, 8, B), F32),
                 vmem((16, B), F32),
                 vmem((probe, 16, B), F32),
                 vmem((CL, 3, 8, B), F32),
                 vmem((CL, 3, 8, B), F32),
+                vmem((CL * (CL + 1) // 2, 2 * ROWS, B), F32),
                 vmem((40, B), F32),
                 vmem((40, B), F32),
                 vmem((2, CL, B, B), BF16),
@@ -592,8 +648,8 @@
                 dma((ORDER, 2)),
                 dma((small,)),
                 dma((small,)),
-                dma((small,)),
-                dma((small,)),
+                dma((clus,)),
+                dma((clus,)),
                 dma((probe,)),
                 dma((probe,)),
                 dma((1,)),
@@ -602,6 +658,7 @@
                 dma((probe,)),
                 dma((probe,)),
                 dma((probe,)),
+                pltpu.SemaphoreType.REGULAR((4,)),
             ],
             compiler_params=pltpu.CompilerParams(
                 collective_id=0, has_side_effects=True, vmem_limit_bytes=60 * 1024 * 1024

time: 49.2 us -> 47.6 us (0.967)
  Pallas kernels: 47.5 us -> 46.1 us
    pallas_call x1, Pallas kernels: 45.3 us -> 43.9 us  [local(): pl.pallas_call(functools.partial(kernel, clus, probe), out_shape=shapes,...]
where the time goes in v3:
time: 47.6 us; the launch traced here: 47.3 us
  Pallas kernels  46.1 us (97%)
  between operations  1.29 us (3%)
    pallas_call x1, Pallas kernels, local(): pl.pallas_call(functools.partial(kernel, clus, probe), out_shape=shapes,...  43.9 us
    pallas_call x1, Pallas kernels, local(): pl.pallas_call(hand_over, out_shape=shapes, in_specs=[in_hbm] * 3, out_sp...  2.13 us

profile of v3, /device:TPU:6, one launch (start us, length us, event | category | flops | bytes accessed | tf_op | source)
XLA Modules:
  0.0 47.3 jit_solution(11987089966723553498)
XLA Ops:
  1.3 43.9 %fermi_forces.1 = (f32[12,128]{1,0:T(8,128)}, f32[1]{0:T(128)}, f32[3,384]{1,0:T(4,128)}) custom-call(bf16[12,16,128]{2,1,0:T(8,128)(2,1)} %probes_hbm.1, f32[12,128]{1,0:T(8,128)} %onsite_hbm.1, bf16[20,12,128,128]{3,2,1,0:T(8,128)(2,1)} %hop_ref.1, s32[12,20]{1,0:T(8,128)} %bitcast.3, s32[12,128]{1,0:T(8,128)} %atom_hbm.1, bf16[3,12,20]{2,1,0:T(8,128)(2,1)} %bitcast.2, ...), custom_call_target="tpu_custom_call" | custom-call | flops 2600000000 | bytes 8500000 | tf_op jit(solution)/shard_map/fermi_forces/pallas_call | solution.py:593
  45.2 2.1 %hand_over.1 = (f32[12,128]{1,0:T(8,128)}, f32[1]{0:T(128)}, f32[3,384]{1,0:T(4,128)}) custom-call(f32[12,128]{1,0:T(8,128)} %get-tuple-element.6.density, f32[1]{0:T(128)} %get-tuple-element.7.filling, f32[3,384]{1,0:T(4,128)} %get-tuple-element.8.forces), custom_call_target="tpu_custom_call" | custom-call | tf_op jit(solution)/shard_map/hand_over/pallas_call | solution.py:672

commit v4 on v3

--- a/solution.py
+++ b/solution.py
@@ -36,9 +36,9 @@
 
 def kernel(
     clus, probe, probes_hbm, onsite_hbm, hop_ref, col_hbm, atom_hbm, bond_hbm, mu_hbm, cos_hbm,
-    density_hbm, filling_hbm, forces_hbm,
-    density_ref, filling_ref, forces_ref, mu_ref, probes_ref, onsite_ref, col_ref, atom_ref, bond_ref, cos_ref, atom_far, kbuf, ktbuf, tab_v, bond_v, tab, bond, xs, halo, part_out, part_in, cheb, fermi, y_acc, coef,
-    norm_buf, norm_in, fill_buf, fill_in, dens_out, dens_in, force_acc, far_acc, ahead, col_out, col_in, onehot, z_out, z_in, f_out, f_in,
+    density_hbm, z_in, f_in, fill_in,
+    density_ref, mu_ref, probes_ref, onsite_ref, col_ref, atom_ref, bond_ref, cos_ref, atom_far, kbuf, ktbuf, tab_v, bond_v, tab, bond, xs, halo, part_out, part_in, cheb, fermi, y_acc, coef,
+    norm_buf, norm_in, fill_buf, dens_out, dens_in, force_acc, far_acc, ahead, col_out, col_in, onehot, z_out, f_out,
     isem, osem, ksem, tsem, asem, hs, hr, ps, pr, ns, nr, gs, gr, ds, dr, fs, fr, zs, zr, ws, wr, word,
 ):
     me = lax.axis_index("clus")
@@ -129,7 +129,6 @@
 
     @pl.when(jnp.logical_not(has_far))
     def _():
-        f_in[...] = jnp.zeros(f_in.shape, F32)
         atom_far[...] = jnp.zeros(atom_far.shape, jnp.int32)
         halo[:, FAR] = jnp.zeros((ORDER + 1, CL, ROWS, B), BF16)
         part_in[:, FAR] = jnp.zeros((ORDER, CL, ROWS, B), LINK)
@@ -246,11 +245,12 @@
     partials(0)
 
     def turn(m, carry):
-        for c in range(CL):
-            ktbuf[m * CL + c] = kbuf[m * CL + c].T
+        for i in range(5):
+            for c in range(CL):
+                ktbuf[(5 * m + i) * CL + c] = kbuf[(5 * m + i) * CL + c].T
         return carry
 
-    lax.fori_loop(0, SLOTS, turn, 0)
+    lax.fori_loop(0, SLOTS // 5, turn, 0)
     collect(norm_copies, norm_buf, norm_in, 0)
 
     def apply(k, carry):
@@ -495,36 +495,25 @@
     summed = z_sum(dens_out, dens_in, ds, dr)
     for c in range(CL):
         density_ref[pl.ds(place[c], 1), :] = summed[c : c + 1, :]
+    fill_buf[...] = summed[0:8] + summed[8:16]
+    for copy in fill_copies():
+        copy.start()
     results = [
         pltpu.make_async_copy(source, target, osem.at[i])
         for i, (source, target) in enumerate(
-            ((density_ref, density_hbm), (forces_ref, forces_hbm), (filling_ref, filling_hbm))
+            ((density_ref, density_hbm), (fill_buf, fill_in.at[me]), (z_out, z_in.at[z]))
         )
     ]
-    results[0].start()
-    fill_buf[...] = summed[0:8] + summed[8:16]
-    for copy in fill_copies():
+    for copy in results:
         copy.start()
-    fill_in[me] = fill_buf[...]
 
     @pl.when(has_far)
     def _():
         for copy in far_copies(True):
             copy.wait_recv()
 
-    summed = z_sum(z_out, z_in, zs, zr)
-    for q in range(probe):
-        summed = summed + f_in[q]
-    for quad in range(CL // 4):
-        forces_ref[:, quad * B : (quad + 1) * B] = summed[quad * 3 : quad * 3 + 3]
-    results[1].start()
-    for copy in fill_copies(True):
+    for copy in z_copies(z_out, z_in, zs, zr, True) + fill_copies(True):
         copy.wait_recv()
-    filled = fill_in[0]
-    for q in range(1, clus):
-        filled = filled + fill_in[q]
-    filling_ref[0] = jnp.sum(filled) / (clus * CL * B)
-    results[2].start()
 
     def finish(k, carry):
         halo_copy(k, NEAR).wait_send()
@@ -559,15 +548,54 @@
         copy.wait()
 
 
-def hand_over(density, filling, forces, density_out, filling_out, forces_out, sems):
-    copies = [
-        pltpu.make_async_copy(source, target, sems.at[i])
-        for i, (source, target) in enumerate(((density, density_out), (filling, filling_out), (forces, forces_out)))
+def combine(
+    clus, probe, density_in, z_hbm, f_hbm, fill_hbm, density_out, filling_out, forces_out,
+    z_in, f_in, fill_in, forces, filling, sems,
+):
+    me = lax.axis_index("clus")
+    has_far = jnp.logical_and(me > 0, me < clus - 1)
+    arrivals = ((z_hbm, z_in), (fill_hbm, fill_in), (density_in, density_out))
+    z_copy, fill_copy, density_copy = [
+        pltpu.make_async_copy(source, target, sems.at[i]) for i, (source, target) in enumerate(arrivals)
     ]
-    for copy in copies:
-        copy.start()
-    for copy in copies:
-        copy.wait()
+    f_copy = pltpu.make_async_copy(f_hbm, f_in, sems.at[3])
+
+    @pl.when(has_far)
+    def _():
+        f_copy.start()
+
+    @pl.when(jnp.logical_not(has_far))
+    def _():
+        f_in[...] = jnp.zeros(f_in.shape, F32)
+
+    z_copy.start()
+    fill_copy.start()
+    density_copy.start()
+
+    @pl.when(has_far)
+    def _():
+        f_copy.wait()
+
+    z_copy.wait()
+    summed = z_in[0]
+    for q in range(1, probe):
+        summed = summed + z_in[q]
+    for q in range(probe):
+        summed = summed + f_in[q]
+    for quad in range(CL // 4):
+        forces[:, quad * B : (quad + 1) * B] = summed[quad * 3 : quad * 3 + 3]
+    forces_copy = pltpu.make_async_copy(forces, forces_out, sems.at[4])
+    forces_copy.start()
+    fill_copy.wait()
+    filled = fill_in[0]
+    for q in range(1, clus):
+        filled = filled + fill_in[q]
+    filling[0] = jnp.sum(filled) / (clus * CL * B)
+    filling_copy = pltpu.make_async_copy(filling, filling_out, sems.at[5])
+    filling_copy.start()
+    density_copy.wait()
+    forces_copy.wait()
+    filling_copy.wait()
 
 
 def cosines():
@@ -592,13 +620,16 @@
         )
         found = pl.pallas_call(
             functools.partial(kernel, clus, probe),
-            out_shape=shapes,
+            out_shape=(
+                jax.ShapeDtypeStruct((CL, B), F32),
+                jax.ShapeDtypeStruct((probe, 16, B), F32),
+                jax.ShapeDtypeStruct((probe, 16, B), F32),
+                jax.ShapeDtypeStruct((clus, 8, B), F32),
+            ),
             in_specs=[in_hbm] * 8,
-            out_specs=(in_hbm,) * 3,
+            out_specs=(in_hbm,) * 4,
             scratch_shapes=[
                 vmem((CL, B), F32),
-                pltpu.SMEM((1,), F32),
-                vmem((3, CL * ATOMS), F32),
                 pltpu.SMEM((1,), F32),
                 vmem((CL, ROWS, B), BF16),
                 vmem((CL, B), F32),
@@ -624,7 +655,6 @@
                 vmem((3, ROWS, B), F32),
                 vmem((small, ROWS, B), F32),
                 vmem((8, B), F32),
-                vmem((clus, 8, B), F32),
                 vmem((16, B), F32),
                 vmem((probe, 16, B), F32),
                 vmem((CL, 3, 8, B), F32),
@@ -634,9 +664,7 @@
                 vmem((40, B), F32),
                 vmem((2, CL, B, B), BF16),
                 vmem((16, B), F32),
-                vmem((probe, 16, B), F32),
                 vmem((16, B), F32),
-                vmem((probe, 16, B), F32),
                 dma((7,)),
                 dma((3,)),
                 dma((SLOTS,)),
@@ -670,13 +698,20 @@
             jnp.asarray(cosines()),
         )
         return pl.pallas_call(
-            hand_over,
+            functools.partial(combine, clus, probe),
             out_shape=shapes,
-            in_specs=[in_hbm] * 3,
+            in_specs=[in_hbm] * 4,
             out_specs=(in_hbm,) * 3,
-            scratch_shapes=[dma((3,))],
+            scratch_shapes=[
+                vmem((probe, 16, B), F32),
+                vmem((probe, 16, B), F32),
+                vmem((clus, 8, B), F32),
+                vmem((3, CL * ATOMS), F32),
+                pltpu.SMEM((1,), F32),
+                dma((6,)),
+            ],
             compiler_params=pltpu.CompilerParams(vmem_limit_bytes=60 * 1024 * 1024),
-            name="hand_over",
+            name="combine",
         )(*found)
 
     return jax.shard_map(

time: 47.6 us -> 46.1 us (0.968)
  Pallas kernels: 46.1 us -> 44.4 us
    pallas_call x2, Pallas kernels: 46.1 us -> 44.4 us  [the longest x1 42.7 us: local(): pl.pallas_call(functools.partial(kernel, clus, probe), out_shape=(jax.Sha...]
where the time goes in v4:
time: 46.1 us; the launch traced here: 45.7 us
  Pallas kernels  44.4 us (96%)
  between operations  1.29 us (3%)
    pallas_call x1, Pallas kernels, local(): pl.pallas_call(functools.partial(kernel, clus, probe), out_shape=(jax.Sha...  42.7 us
    pallas_call x1, Pallas kernels, local(): pl.pallas_call(functools.partial(combine, clus, probe), out_shape=shapes,...  1.71 us

profile of v4, /device:TPU:6, one launch (start us, length us, event | category | flops | bytes accessed | tf_op | source)
XLA Modules:
  0.0 45.7 jit_solution(1861829861319031304)
XLA Ops:
  1.3 42.7 %fermi_forces.1 = (f32[12,128]{1,0:T(8,128)}, f32[8,16,128]{2,1,0:T(8,128)}, f32[8,16,128]{2,1,0:T(8,128)}, f32[32,8,128]{2,1,0:T(8,128)}) custom-call(bf16[12,16,128]{2,1,0:T(8,128)(2,1)} %probes_hbm.1, f32[12,128]{1,0:T(8,128)} %onsite_hbm.1, bf16[20,12,128,128]{3,2,1,0:T(8,128)(2,1)} %hop_ref.1, s32[12,20]{1,0:T(8,128)} %bitcast.3, s32[12,128]{1,0:T(8,128)} %atom_hbm.1, ...), custom_call_target="tpu_custom_call" | custom-call | flops 2600000000 | bytes 8500000 | tf_op jit(solution)/shard_map/fermi_forces/pallas_call | solution.py:621
  44.0 1.7 %combine.1 = (f32[12,128]{1,0:T(8,128)}, f32[1]{0:T(128)}, f32[3,384]{1,0:T(4,128)}) custom-call(f32[12,128]{1,0:T(8,128)} %get-tuple-element.7.density_in, f32[8,16,128]{2,1,0:T(8,128)} %get-tuple-element.8.z_hbm, f32[8,16,128]{2,1,0:T(8,128)} %get-tuple-element.9.f_hbm, f32[32,8,128]{2,1,0:T(8,128)} %get-tuple-element.10.fill_hbm), custom_call_target="tpu_custom_call" | custom-call | tf_op jit(solution)/shard_map/combine/pallas_call | solution.py:700

commit v5 on v4

--- a/solution.py
+++ b/solution.py
@@ -158,6 +158,10 @@
     def part_copy(k, side):
         return send(part_out.at[k, side], part_in.at[k, side], ps.at[k, side], pr.at[k, side], (far, near)[side])
 
+    def far_first(copies, first):
+        order = sorted(range(len(copies)), key=lambda i: abs(i + first - probe // 2))
+        return [copies[i] for i in order]
+
     def stage_copies(own, arrived, s, r, stage, arriving=False):
         if stage == 0:
             return [send(own.at[0], arrived.at[chips], s.at[0], r.at[chips], near)]
@@ -346,7 +350,7 @@
         for q, peer in enumerate(z_peers):
             slot = (z + probe - q - 1) % probe if arriving else z
             copies.append(send(src, dst.at[slot], s.at[q], r.at[slot], peer))
-        return copies
+        return far_first(copies, 1)
 
     def z_sum(src, dst, s, r):
         dst[z] = src[...]
@@ -427,7 +431,7 @@
         for q, peer in enumerate(far_peers):
             place_in = (z + probe - q) % probe if arriving else z
             copies.append(send(f_out, f_in.at[place_in], ws.at[q], wr.at[place_in], peer))
-        return copies
+        return far_first(copies, 0)
 
     def halo_both(side, b):
         return jnp.concatenate([halo[0, side, b], halo[ORDER, side, b]], axis=0)

time: 46.1 us -> 45.6 us (0.989)
  no operation moved by 1% of the time
where the time goes in v5:
time: 45.6 us; the launch traced here: 45.4 us
  Pallas kernels  44.2 us (97%)
  between operations  1.29 us (3%)
    pallas_call x1, Pallas kernels, local(): pl.pallas_call(functools.partial(kernel, clus, probe), out_shape=(jax.Sha...  42.5 us
    pallas_call x1, Pallas kernels, local(): pl.pallas_call(functools.partial(combine, clus, probe), out_shape=shapes,...  1.71 us

profile of v5, /device:TPU:6, one launch (start us, length us, event | category | flops | bytes accessed | tf_op | source)
XLA Modules:
  0.0 45.4 jit_solution(1372579495962409575)
XLA Ops:
  1.3 42.5 %fermi_forces.1 = (f32[12,128]{1,0:T(8,128)}, f32[8,16,128]{2,1,0:T(8,128)}, f32[8,16,128]{2,1,0:T(8,128)}, f32[32,8,128]{2,1,0:T(8,128)}) custom-call(bf16[12,16,128]{2,1,0:T(8,128)(2,1)} %probes_hbm.1, f32[12,128]{1,0:T(8,128)} %onsite_hbm.1, bf16[20,12,128,128]{3,2,1,0:T(8,128)(2,1)} %hop_ref.1, s32[12,20]{1,0:T(8,128)} %bitcast.3, s32[12,128]{1,0:T(8,128)} %atom_hbm.1, ...), custom_call_target="tpu_custom_call" | custom-call | flops 2600000000 | bytes 8500000 | tf_op jit(solution)/shard_map/fermi_forces/pallas_call | solution.py:625
  43.7 1.7 %combine.1 = (f32[12,128]{1,0:T(8,128)}, f32[1]{0:T(128)}, f32[3,384]{1,0:T(4,128)}) custom-call(f32[12,128]{1,0:T(8,128)} %get-tuple-element.7.density_in, f32[8,16,128]{2,1,0:T(8,128)} %get-tuple-element.8.z_hbm, f32[8,16,128]{2,1,0:T(8,128)} %get-tuple-element.9.f_hbm, f32[32,8,128]{2,1,0:T(8,128)} %get-tuple-element.10.fill_hbm), custom_call_target="tpu_custom_call" | custom-call | tf_op jit(solution)/shard_map/combine/pallas_call | solution.py:704

commit v6 on v5

--- a/solution.py
+++ b/solution.py
@@ -249,12 +249,12 @@
     partials(0)
 
     def turn(m, carry):
-        for i in range(5):
+        for i in range(10):
             for c in range(CL):
-                ktbuf[(5 * m + i) * CL + c] = kbuf[(5 * m + i) * CL + c].T
+                ktbuf[(10 * m + i) * CL + c] = kbuf[(10 * m + i) * CL + c].T
         return carry
 
-    lax.fori_loop(0, SLOTS // 5, turn, 0)
+    lax.fori_loop(0, SLOTS // 10, turn, 0)
     collect(norm_copies, norm_buf, norm_in, 0)
 
     def apply(k, carry):

time: 45.6 us -> 45.4 us (level)
  no operation moved by 1% of the time
where the time goes in v6:
time: 45.4 us; the launch traced here: 45.3 us
  Pallas kernels  44.1 us (97%)
  between operations  1.29 us (3%)
    pallas_call x1, Pallas kernels, local(): pl.pallas_call(functools.partial(kernel, clus, probe), out_shape=(jax.Sha...  42.3 us
    pallas_call x1, Pallas kernels, local(): pl.pallas_call(functools.partial(combine, clus, probe), out_shape=shapes,...  1.71 us

profile of v6, /device:TPU:6, one launch (start us, length us, event | category | flops | bytes accessed | tf_op | source)
XLA Modules:
  0.0 45.3 jit_solution(16511387786897030513)
XLA Ops:
  1.3 42.3 %fermi_forces.1 = (f32[12,128]{1,0:T(8,128)}, f32[8,16,128]{2,1,0:T(8,128)}, f32[8,16,128]{2,1,0:T(8,128)}, f32[32,8,128]{2,1,0:T(8,128)}) custom-call(bf16[12,16,128]{2,1,0:T(8,128)(2,1)} %probes_hbm.1, f32[12,128]{1,0:T(8,128)} %onsite_hbm.1, bf16[20,12,128,128]{3,2,1,0:T(8,128)(2,1)} %hop_ref.1, s32[12,20]{1,0:T(8,128)} %bitcast.3, s32[12,128]{1,0:T(8,128)} %atom_hbm.1, ...), custom_call_target="tpu_custom_call" | custom-call | flops 2600000000 | bytes 8500000 | tf_op jit(solution)/shard_map/fermi_forces/pallas_call | solution.py:625
  43.6 1.7 %combine.1 = (f32[12,128]{1,0:T(8,128)}, f32[1]{0:T(128)}, f32[3,384]{1,0:T(4,128)}) custom-call(f32[12,128]{1,0:T(8,128)} %get-tuple-element.7.density_in, f32[8,16,128]{2,1,0:T(8,128)} %get-tuple-element.8.z_hbm, f32[8,16,128]{2,1,0:T(8,128)} %get-tuple-element.9.f_hbm, f32[32,8,128]{2,1,0:T(8,128)} %get-tuple-element.10.fill_hbm), custom_call_target="tpu_custom_call" | custom-call | tf_op jit(solution)/shard_map/combine/pallas_call | solution.py:704
